TPU v7x, 256 devices: a whole 4x4x8 slice. The times are simulated.
256 devices in a mesh: row: 16 (over x, y_lo, core), col: 16 (over y_hi, z).
Axes of the slice: x: 4, y: 4 (y_hi: 2, y_lo: 2; y = y_hi * 2 + y_lo), z: 8, core: 2. Of those that a mesh axis runs over, the one named last changes fastest.
Arguments:
- pair: bfloat16 [512, 512, 128], P('row', 'col'), may hold values from -6 to 6
- gain_in: float32 [128], replicated, may hold values from 0.1 to 1.9
- in_weight: bfloat16 [128, 640], replicated, may hold values from -0.5 to 0.5
- gain_out: float32 [128], replicated, may hold values from 0.1 to 1.9
- out_weight: bfloat16 [128, 128], replicated, may hold values from -0.5 to 0.5
- out_grad: bfloat16 [512, 512, 128], P('row', 'col'), may hold values from -6 to 6
Outputs:
- update: bfloat16 [512, 512, 128], P('row', 'col')
- pair_grad: float32 [512, 512, 128], P('row', 'col')
- in_weight_grad: float32 [128, 640], replicated
- out_weight_grad: float32 [128, 128], replicated
- gain_grad: float32 [2, 128], replicated
All inputs are finite; a program needn't handle non-finite values.
Results may differ from a plain program's by a relative error of at most 0.017.
Values may be sent and summed in bfloat16 or wider, within the bound.
A program may use at most 128 MiB of HBM per device.

v0:
```python
import jax
import jax.numpy as jnp
from jax import lax
from jax.sharding import PartitionSpec as P

epsilon = 1e-05


def layer_norm(values, gain):
    average = jnp.mean(values, axis=-1, keepdims=True)
    centred = values - average
    variance = jnp.mean(centred * centred, axis=-1, keepdims=True)
    return centred * lax.rsqrt(variance + epsilon) * gain


def edge_gates(projected):
    width = projected.shape[-1] // 5
    parts = [projected[:, index * width : (index + 1) * width] for index in range(5)]
    left_edge = jax.nn.sigmoid(parts[0]) * parts[1]
    right_edge = jax.nn.sigmoid(parts[2]) * parts[3]
    gate_value = jax.nn.sigmoid(parts[4])
    return (left_edge, right_edge, gate_value)


def on_device(pair, gain_in, in_weight, gain_out, out_weight, out_grad):
    tile_rows, tile_cols, channels = pair.shape
    cell_count = tile_rows * tile_cols
    cells_in = pair.astype(jnp.float32).reshape(cell_count, channels)
    normed_in, in_back = jax.vjp(layer_norm, cells_in, gain_in)
    normed_bf = normed_in.astype(jnp.bfloat16)
    projected = jnp.dot(normed_bf, in_weight, preferred_element_type=jnp.float32)
    left_edge, right_edge, gate_value = edge_gates(projected)
    left_bf = left_edge.astype(jnp.bfloat16).reshape(tile_rows, tile_cols, channels)
    right_bf = right_edge.astype(jnp.bfloat16).reshape(tile_rows, tile_cols, channels)
    right_whole = lax.all_gather(right_bf, "row", axis=0, tiled=True)
    pair_term = jnp.einsum("ikc,jkc->ijc", left_bf, right_whole, preferred_element_type=jnp.float32)
    mixed = lax.psum_scatter(pair_term, "col", scatter_dimension=1, tiled=True)
    cells_mixed = mixed.reshape(cell_count, channels)
    normed_out, out_back = jax.vjp(layer_norm, cells_mixed, gain_out)
    normed_out_bf = normed_out.astype(jnp.bfloat16)
    projected_out = jnp.dot(normed_out_bf, out_weight, preferred_element_type=jnp.float32)
    update = (
        (gate_value * projected_out).astype(jnp.bfloat16).reshape(tile_rows, tile_cols, channels)
    )
    cotangent = out_grad.astype(jnp.float32).reshape(cell_count, channels)
    grad_proj_out = (cotangent * gate_value).astype(jnp.bfloat16)
    grad_gate = cotangent * projected_out
    out_weight_part = jnp.einsum(
        "mc,md->cd", normed_out_bf, grad_proj_out, preferred_element_type=jnp.float32
    )
    grad_normed_out = jnp.dot(grad_proj_out, out_weight.T, preferred_element_type=jnp.float32)
    grad_mixed, gain_out_part = out_back(grad_normed_out)
    grad_mixed_bf = grad_mixed.astype(jnp.bfloat16).reshape(tile_rows, tile_cols, channels)
    grad_whole = lax.all_gather(grad_mixed_bf, "col", axis=1, tiled=True)
    grad_left = jnp.einsum(
        "ijc,jkc->ikc", grad_whole, right_whole, preferred_element_type=jnp.float32
    )
    right_term = jnp.einsum("ijc,ikc->jkc", grad_whole, left_bf, preferred_element_type=jnp.float32)
    grad_right = lax.psum_scatter(
        right_term.astype(jnp.bfloat16), "row", scatter_dimension=0, tiled=True
    ).astype(jnp.float32)
    gate_outputs, gate_back = jax.vjp(edge_gates, projected)
    grad_projected = gate_back(
        (
            grad_left.reshape(cell_count, channels),
            grad_right.reshape(cell_count, channels),
            grad_gate,
        )
    )[0]
    grad_projected_bf = grad_projected.astype(jnp.bfloat16)
    in_weight_part = jnp.einsum(
        "mc,md->cd", normed_bf, grad_projected_bf, preferred_element_type=jnp.float32
    )
    grad_normed_in = jnp.dot(grad_projected_bf, in_weight.T, preferred_element_type=jnp.float32)
    pair_grad, gain_in_part = in_back(grad_normed_in)
    in_weight_grad, out_weight_grad, gain_grad = lax.psum(
        (in_weight_part, out_weight_part, jnp.stack([gain_in_part, gain_out_part])), ("row", "col")
    )
    return (
        update,
        pair_grad.reshape(tile_rows, tile_cols, channels),
        in_weight_grad,
        out_weight_grad,
        gain_grad,
    )


def solution(mesh):
    return jax.shard_map(
        on_device,
        mesh=mesh,
        in_specs=(P("row", "col", None), P(), P(), P(), P(), P("row", "col", None)),
        out_specs=(P("row", "col", None), P("row", "col", None), P(), P(), P()),
        check_vma=False,
    )
```

profile of v0, /device:TPU:1, one launch (start us, length us, event | category | flops | bytes accessed | tf_op | source)
XLA Modules:
  0.0 893.8 jit_solution(1476227209129812485)
XLA Ops:
  8.5 1.3 multiply_reduce_fusion.5
  9.9 1.3 multiply_convert_fusion.4
  13.0 3.2 copy.67
  16.3 2.6 copy.75
  18.9 95.8 %all-gather.3.cloned.1.call-done = bf16[512,32,128]{1,0,2:T(8,128)(2,1)} async-done(((bf16[32,32,128]{1,0,2:T(8,128)(2,1)}), bf16[512,32,128]{1,0,2:T(8,128)(2,1)}) %all-gather.3.cloned.1.call-update) | async-done | bytes 4194320 | tf_op jit(solution)/shard_map/all_gather | solution.py:35
  114.7 11.5 %convolution_bitcast_fusion = f32[32,512,128]{1,0,2:T(8,128)} fusion(bf16[512,32,128]{1,0,2:T(8,128)(2,1)} %all-gather.3.cloned.1.call-done, bf16[32,32,128]{0,1,2:T(8,128)(2,1)} %copy.75), kind=kOutput, calls=%fused_computation.1 | convolution fusion | flops 134217728 | bytes 12845056 | tf_op jit(solution)/shard_map/ikc,jkc->ijc/dot_general | solution.py:36
  126.2 11.0 %copy.69 = f32[32,512,128]{2,0,1:T(8,128)} copy(f32[32,512,128]{1,0,2:T(8,128)} %convolution_bitcast_fusion) | data formatting | bytes 16777216 | tf_op jit(solution)/shard_map/ikc,jkc->ijc/transpose | solution.py:36
  137.3 219.4 %reduce-scatter.3.cloned.1.call-done = f32[32,32,128]{2,0,1:T(8,128)} async-done(((f32[32,512,128]{2,0,1:T(8,128)}), f32[32,32,128]{2,0,1:T(8,128)}) %reduce-scatter.3.cloned.1.call-update) | async-done | bytes 524304 | tf_op jit(solution)/shard_map/reduce_scatter | solution.py:37
  358.1 1.4 multiply_reduce_fusion.4
  359.7 1.4 copy.70
  361.5 2.2 fusion
  366.4 99.3 %all-gather.5.cloned.1.call-done = bf16[32,512,128]{2,0,1:T(8,128)(2,1)} async-done(((bf16[32,32,128]{2,0,1:T(8,128)(2,1)}), bf16[32,512,128]{2,0,1:T(8,128)(2,1)}) %all-gather.5.cloned.1.call-update) | async-done | bytes 4194320 | tf_op jit(solution)/shard_map/all_gather | solution.py:54
  465.7 8.6 copy.76
  474.2 5.4 convert_bitcast_fusion
  479.6 9.1 %copy.77 = bf16[512,32,128]{2,1,0:T(8,128)(2,1)} copy(bf16[512,32,128]{0,1,2:T(8,128)(2,1)} %convert_bitcast_fusion) | data formatting | bytes 8388608 | tf_op jit(solution)/shard_map/convert_element_type | solution.py:60
  490.6 9.3 %convolution_bitcast_fusion.1 = f32[32,32,128]{0,1,2:T(8,128)S(1)} fusion(bf16[512,32,128]{1,0,2:T(8,128)(2,1)} %all-gather.3.cloned.1.call-done, bf16[32,512,128]{1,0,2:T(8,128)(2,1)} %copy.76), kind=kOutput, calls=%fused_computation.3 | convolution fusion | flops 134217728 | bytes 8912896 | tf_op jit(solution)/shard_map/ijc,jkc->ikc/dot_general | solution.py:55
  499.9 1.4 copy.80
  501.3 54.2 %reduce-scatter.5.cloned.1.call-done = bf16[32,32,128]{2,1,0:T(8,128)(2,1)} async-done(((bf16[512,32,128]{2,1,0:T(8,128)(2,1)}), bf16[32,32,128]{2,1,0:T(8,128)(2,1)}) %reduce-scatter.5.cloned.1.call-update) | async-done | bytes 262160 | tf_op jit(solution)/shard_map/reduce_scatter | solution.py:59
  555.5 2.0 convert_multiply_fusion.1
  560.1 79.0 %psum.23 = f32[2,128]{1,0:T(2,128)} all-reduce(f32[2,128]{1,0:T(2,128)S(1)} %pad_maximum_fusion), channel_id=1, replica_groups=mesh['row'=16,'col'=16] {'row','col'}, use_global_device_ids=true, to_apply=%region_14.0 | all-reduce | flops 256 | bytes 2048 | tf_op jit(solution)/shard_map/psum | solution.py:76
  639.1 1.4 broadcast_add_fusion
  640.5 243.5 %all-reduce.8.cloned.1.call-done = (f32[128,640]{1,0:T(8,128)}, f32[128,128]{1,0:T(8,128)}) async-done(((f32[128,640]{1,0:T(8,128)}, f32[128,128]{1,0:T(8,128)}), (f32[128,640]{1,0:T(8,128)}, f32[128,128]{1,0:T(8,128)})) %all-reduce.8.cloned.1.call-update) | async-done | bytes 393232 | tf_op jit(solution)/shard_map/psum | solution.py:76
  884.0 1.7 copy.84
  885.8 1.5 copy.85
  (62 shorter events, 12.4 us)
Async XLA Ops:
  7.2 4.1 copy-start
  7.2 107.6 %all-gather.3.cloned.1.call-start = ((), (), s32[]{:S(2)}) async-start(), calls=%async_computation.2 | async-start | bytes 17825792 | tf_op jit(solution)/shard_map/all_gather | solution.py:35
  11.7 349.7 %copy-start.1 = (f32[1024,640]{1,0:T(8,128)}, f32[1024,640]{1,0:T(8,128)S(1)}, u32[]{:S(2)}) copy-start(f32[1024,640]{1,0:T(8,128)S(1)} %fusion.15) | copy-start | bytes 7864324
  16.3 340.4 %reduce-scatter.3.cloned.1.call-start = ((), (), s32[]{:S(2)}) async-start(), calls=%async_computation.3 | async-start | bytes 8912896 | tf_op jit(solution)/shard_map/reduce_scatter | solution.py:37
  137.2 223.9 %copy-start.9 = (f32[128]{0:T(128)S(1)}, f32[128]{0:T(128)}, u32[]{:S(2)}) copy-start(f32[128]{0:T(128)} %param.9) | copy-start | bytes 1540
  137.2 224.2 %copy-start.7 = (bf16[128,128]{1,0:T(8,128)(2,1)S(1)}, bf16[128,128]{1,0:T(8,128)(2,1)}, u32[]{:S(2)}) copy-start(bf16[128,128]{1,0:T(8,128)(2,1)} %param.10) | copy-start | bytes 98308
  137.2 328.4 %all-gather.5.cloned.1.call-start = ((), (), s32[]{:S(2)}) async-start(), calls=%async_computation.4 | async-start | bytes 4456448 | tf_op jit(solution)/shard_map/all_gather | solution.py:54
  363.6 1.0 copy-start.4
  366.3 107.9 %copy-start.2 = (bf16[32,32,128]{0,1,2:T(8,128)(2,1)S(1)}, bf16[32,32,128]{0,1,2:T(8,128)(2,1)}, u32[]{:S(2)}) copy-start(bf16[32,32,128]{0,1,2:T(8,128)(2,1)} %copy.75) | copy-start | bytes 786436
  366.4 189.2 %reduce-scatter.5.cloned.1.call-start = ((), (), s32[]{:S(2)}) async-start(), calls=%async_computation.5 | async-start | bytes 4456448 | tf_op jit(solution)/shard_map/reduce_scatter | solution.py:59
  488.8 0.9 copy-start.5
  488.8 395.3 %all-reduce.8.cloned.1.call-start = ((), (), s32[]{:S(2)}) async-start(), calls=%async_computation.6 | async-start | bytes 786432 | tf_op jit(solution)/shard_map/psum | solution.py:76
  555.5 2.0 copy-start.6
  557.5 1.3 copy-start.3
  557.6 1.3 copy-start.8
Sparse Core Ops, SparseCore 0:
  16.4 98.3 all-gather.2
  137.3 219.2 reduce-scatter.2
  366.5 99.1 all-gather.4
  488.9 66.5 reduce-scatter.4
  639.2 244.7 all-reduce.7
where the time goes:
time: 895 us; the launch traced here: 894 us
  waiting for transfers between devices  712 us (80%)
  blocking collectives  79 us (9%)
  local copies, waits for them, and re-layouts  42.6 us (5%)
  matrix products  32.4 us (4%)
  between operations  14 us (2%)
  other arithmetic  13.2 us (1%)
    psum x1, waiting for transfers between devices, on_device(): lax.psum((in_weight_part, out_weight_part, jnp.stack([gain_in_part, gain_...  244 us
    reduce_scatter x1, waiting for transfers between devices, on_device(): mixed = lax.psum_scatter(pair_term, 'col', scatter_dimension=1, tiled=True)  219 us
    all_gather x1, waiting for transfers between devices, on_device(): grad_whole = lax.all_gather(grad_mixed_bf, 'col', axis=1, tiled=True)  99.3 us
    all_gather x1, waiting for transfers between devices, on_device(): right_whole = lax.all_gather(right_bf, 'row', axis=0, tiled=True)  95.8 us
    psum x1, blocking collectives, on_device(): lax.psum((in_weight_part, out_weight_part, jnp.stack([gain_in_part, gain_...  79 us
    reduce_scatter x1, waiting for transfers between devices, on_device(): lax.psum_scatter(right_term.astype(jnp.bfloat16), 'row', scatter_dimensio...  54.2 us
  transfers between devices with their start and end apart: 5, of which 5 were waited for; matrix products, arithmetic and copies ran while one was open for 2% of the time, Pallas kernels for 0%

commit v1 on v0

v1 whole, which is shorter than its diff:
```python
import functools

import jax
import jax.numpy as jnp
from jax import lax
from jax.experimental import pallas as pl
from jax.experimental.pallas import tpu as pltpu
from jax.sharding import PartitionSpec as P

EPS = 1e-05
MESH = pl.DeviceIdType.MESH
F32 = jnp.float32
BF16 = jnp.bfloat16
NT = (((1,), (1,)), ((), ()))
TN = (((0,), (0,)), ((), ()))


def dot(a, b, dims=(((1,), (0,)), ((), ()))):
    return lax.dot_general(a, b, dims, preferred_element_type=F32)


def swap_blocks(tiles):
    shape = tiles[0].shape
    flat = [t.reshape(-1, 128) for t in tiles]
    lane = lax.broadcasted_iota(jnp.int32, flat[0].shape, 1)
    low = lane < 64
    even = (lane // 32) % 2 == 0
    half = [None] * 4
    for q in range(2):
        a, b = flat[q], flat[q + 2]
        half[q] = jnp.where(low, a, pltpu.roll(b, 64, 1))
        half[q + 2] = jnp.where(low, pltpu.roll(a, 64, 1), b)
    out = [None] * 4
    for q in (0, 2):
        a, b = half[q], half[q + 1]
        out[q] = jnp.where(even, a, pltpu.roll(b, 32, 1))
        out[q + 1] = jnp.where(even, pltpu.roll(a, 96, 1), b)
    return [t.reshape(shape) for t in out]


def kernel(
    pair, gain_in, weight, gain_out, out_weight, out_grad,
    update_o, pair_grad_o, weight_grad_o, out_weight_grad_o, gain_grad_o,
    wide, sb1, rb1, left32, right32, edges, sb2, rb2, sb3, rb3, grad_mat, grad_far, sb4, rb4,
    normed, hat_in, rstd_in, gates, grad_po, grad_no, og_t, grad_p, w_t, ow_t, g_in, g_out,
    part, part_far, s1, r1, s2, r2, final,
    send, recv, sib_send, sib_recv, red_send, red_recv,
):
    row, col = lax.axis_index("row"), lax.axis_index("col")
    core, rx = row % 2, row // 2
    me = rx * 16 + col
    sibling = (rx * 2 + 1 - core, col)
    barrier = pltpu.get_barrier_semaphore()

    def partner(t):
        r = (rx + t // 16) % 8
        c = (col + t % 16) % 16
        return r, c

    def greet(t, carry):
        r, c = partner(t)
        pl.semaphore_signal(barrier, inc=1, device_id=(r * 2 + core, c), device_id_type=MESH)
        return carry

    lax.fori_loop(1, 128, greet, 0)
    pl.semaphore_signal(barrier, inc=1, device_id=sibling, device_id_type=MESH)

    def exchange(source, target, slot, own_source, own_target):
        def one(t, carry):
            r, c = partner(t)
            pltpu.make_async_remote_copy(
                src_ref=source(r, c), dst_ref=target, send_sem=send.at[slot], recv_sem=recv.at[slot],
                device_id=(r * 2 + core, c), device_id_type=MESH,
            ).start()
            return carry

        lax.fori_loop(1, 128, one, 0)
        own_target[...] = own_source[...]

    def arrive(buffer, semaphore):
        view = buffer.at[pl.ds(0, 127)]
        pltpu.make_async_copy(view, view, semaphore).wait()

    def to_sibling(source, target, slot):
        return pltpu.make_async_remote_copy(
            src_ref=source, dst_ref=target, send_sem=sib_send.at[slot], recv_sem=sib_recv.at[slot],
            device_id=sibling, device_id_type=MESH,
        )

    w_t[...] = weight[...].astype(F32).T.astype(BF16)
    g_in[...] = jnp.broadcast_to(gain_in[...], (128, 128)).T
    for s in range(8):
        lanes = pl.ds(s * 128, 128)
        x = pair[:, s].reshape(128, 128).astype(F32).T
        centred = x - jnp.mean(x, axis=0, keepdims=True)
        rstd = lax.rsqrt(jnp.mean(centred * centred, axis=0, keepdims=True) + EPS)
        hat = centred * rstd
        hat_in[:, lanes] = hat
        rstd_in[:, lanes] = rstd
        n = (hat * g_in[...]).astype(BF16)
        normed[:, lanes] = n
        p = dot(w_t[pl.ds(0, 512)], n)
        s0, p1 = jax.nn.sigmoid(p[0:128]), p[128:256]
        s2_, p3 = jax.nn.sigmoid(p[256:384]), p[384:512]
        gates[0, :, lanes] = s0
        gates[1, :, lanes] = p1
        gates[2, :, lanes] = s2_
        gates[3, :, lanes] = p3
        wide[:, s, :] = s0 * p1
        wide[:, 8 + s, :] = s2_ * p3
    sb1[...] = wide[...].astype(BF16)

    pl.semaphore_wait(barrier, 128)
    exchange(
        lambda r, c: sb1.at[r * 16 + c], rb1.at[rx, col // 4, col % 4], 0,
        sb1.at[me], rb1.at[rx, col // 4, col % 4],
    )

    ow_t[...] = out_weight[...].astype(F32).T.astype(BF16)
    g_out[...] = jnp.broadcast_to(gain_out[...], (128, 128)).T
    for s in range(8):
        lanes = pl.ds(s * 128, 128)
        gate = jax.nn.sigmoid(dot(w_t[pl.ds(512, 128)], normed[:, lanes]))
        gates[4, :, lanes] = gate
        cotangent = out_grad[:, s].reshape(128, 128).astype(F32).T
        og_t[:, lanes] = cotangent
        gpo = (cotangent * gate).astype(BF16)
        grad_po[:, lanes] = gpo
        grad_no[:, lanes] = dot(out_weight[...], gpo)

    arrive(sb1, recv.at[0])
    for g in range(4):
        tiles = [rb1[:, g, q].astype(F32) for q in range(4)]
        for a, tile in enumerate(swap_blocks(tiles)):
            left32[:, a, :, pl.ds(g * 128, 128)] = tile[:, 0:8]
            right32[:, a, :, pl.ds(g * 128, 128)] = tile[:, 8:16]
    edges[0, 0] = left32[...].reshape(256, 512).astype(BF16)
    edges[0, 1] = right32[...].reshape(256, 512).astype(BF16)
    copy_edges = to_sibling(edges.at[0], edges.at[1], 0)
    copy_edges.start()

    def send_mixed(slot):
        mixed = dot(edges[0, 0], edges[slot, 1], NT).reshape(8, 4, 8, 256)
        for g in range(2):
            tiles = swap_blocks([mixed[:, a, :, g * 128 : g * 128 + 128] for a in range(4)])
            for q in range(4):
                sb2[slot, :, g, q] = tiles[q].astype(BF16)

    send_mixed(0)
    copy_edges.wait()
    send_mixed(1)

    def mixed_tile(r, c):
        return sb2.at[(c % 2 + core) % 2, r, c // 8, (c // 2) % 4]

    exchange(mixed_tile, rb2.at[me], 1, mixed_tile(rx, col), rb2.at[me])
    arrive(rb2, recv.at[1])

    wide[:, 0:8, :] = rb2[...].astype(F32)
    gain_sum = jnp.zeros((128, 128), F32)
    for s in range(8):
        lanes = pl.ds(s * 128, 128)
        x = wide[:, s, :]
        centred = x - jnp.mean(x, axis=0, keepdims=True)
        rstd = lax.rsqrt(jnp.mean(centred * centred, axis=0, keepdims=True) + EPS)
        hat = centred * rstd
        gno = grad_no[:, lanes]
        gain_sum = gain_sum + gno * hat
        cot = gno * g_out[...]
        inner = jnp.mean(cot * hat, axis=0, keepdims=True)
        grad = rstd * (cot - jnp.mean(cot, axis=0, keepdims=True) - hat * inner)
        grad_no[:, lanes] = hat
        wide[:, 8 + s, :] = grad
    sb3[...] = wide[:, 8:16, :].astype(BF16)
    here = rb3.at[(col % 2 + core) % 2, rx, col // 8, (col // 2) % 4]
    exchange(lambda r, c: sb3.at[r * 16 + c], here, 2, sb3.at[me], here)
    gain_out_part = jnp.sum(gain_sum.T, axis=0, keepdims=True)

    for s in range(8):
        lanes = pl.ds(s * 128, 128)
        no = (grad_no[:, lanes] * g_out[...]).astype(BF16)
        sb_no = no
        grad_p[pl.ds(0, 128), lanes] = sb_no
        po = dot(ow_t[...], no)
        gate = gates[4, :, lanes]
        update_o[:, s] = (gate * po).T.reshape(4, 32, 128).astype(BF16)
        grad_p[pl.ds(512, 128), lanes] = (og_t[:, lanes] * po * (gate * (1.0 - gate))).astype(BF16)
    out_part = dot(grad_p[pl.ds(0, 128)], grad_po[...], NT)

    arrive(sb3, recv.at[2])
    for slot in range(2):
        for g in range(2):
            tiles = swap_blocks([rb3[slot, :, g, q].astype(F32) for q in range(4)])
            for a in range(4):
                left32[:, a, :, pl.ds(slot * 256 + g * 128, 128)] = tiles[a]
    for slot in range(2):
        grad_mat[slot] = left32[:, :, :, pl.ds(slot * 256, 256)].reshape(256, 256).astype(BF16)
    copy_grad = to_sibling(grad_mat.at[1], grad_far, 1)
    copy_grad.start()
    grad_left = dot(grad_mat[0], edges[0, 1]) + dot(grad_mat[1], edges[1, 1])
    left32[...] = grad_left.reshape(8, 4, 8, 512)
    grad_right = dot(grad_mat[0], edges[0, 0], TN)
    copy_grad.wait()
    grad_right = grad_right + dot(grad_far[...], edges[1, 0], TN)
    right32[...] = grad_right.reshape(8, 4, 8, 512)
    for g in range(4):
        lanes = pl.ds(g * 128, 128)
        tiles = swap_blocks(
            [jnp.concatenate([left32[:, a, :, lanes], right32[:, a, :, lanes]], axis=1) for a in range(4)]
        )
        for q in range(4):
            sb4[:, g, q] = tiles[q].astype(BF16)
    exchange(lambda r, c: sb4.at[r, c // 4, c % 4], rb4.at[me], 3, sb4.at[rx, col // 4, col % 4], rb4.at[me])

    gate_part = dot(normed[...], grad_p[pl.ds(512, 128)], NT)
    arrive(rb4, recv.at[3])
    wide[...] = rb4[...].astype(F32)
    gain_sum = jnp.zeros((128, 128), F32)
    for s in range(8):
        lanes = pl.ds(s * 128, 128)
        gl, gr = wide[:, s, :], wide[:, 8 + s, :]
        s0, p1 = gates[0, :, lanes], gates[1, :, lanes]
        s2_, p3 = gates[2, :, lanes], gates[3, :, lanes]
        dl, dr = gl * s0, gr * s2_
        grad_p[pl.ds(0, 128), lanes] = (dl * p1 * (1.0 - s0)).astype(BF16)
        grad_p[pl.ds(128, 128), lanes] = dl.astype(BF16)
        grad_p[pl.ds(256, 128), lanes] = (dr * p3 * (1.0 - s2_)).astype(BF16)
        grad_p[pl.ds(384, 128), lanes] = dr.astype(BF16)
        gni = dot(weight[...], grad_p[:, lanes])
        gain_sum = gain_sum + gni * hat_in[:, lanes]
        og_t[:, lanes] = gni
    gain_in_part = jnp.sum(gain_sum.T, axis=0, keepdims=True)
    in_part = dot(normed[...], grad_p[pl.ds(0, 512)], NT)
    blocks = [in_part[:, 0:128], in_part[:, 128:256], in_part[:, 256:384]]
    part[0, :, 0:24, :] = jnp.concatenate(blocks, axis=0).reshape(16, 24, 128)
    blocks = [in_part[:, 384:512], gate_part, out_part]
    part[1, :, 0:24, :] = jnp.concatenate(blocks, axis=0).reshape(16, 24, 128)
    index = lax.broadcasted_iota(jnp.int32, (8, 128), 0)
    gain_tile = jnp.where(index == 0, gain_in_part, jnp.where(index == 1, gain_out_part, 0.0))
    part[:, :, 24:32, :] = jnp.broadcast_to(gain_tile[None, None], (2, 16, 8, 128))

    copy_part = to_sibling(part.at[1 - core], part_far, 2)
    copy_part.start()
    for s in range(8):
        lanes = pl.ds(s * 128, 128)
        hat = hat_in[:, lanes]
        cot = og_t[:, lanes] * g_in[...]
        inner = jnp.mean(cot * hat, axis=0, keepdims=True)
        grad = rstd_in[:, lanes] * (cot - jnp.mean(cot, axis=0, keepdims=True) - hat * inner)
        pair_grad_o[:, s] = grad.T.reshape(4, 32, 128)
    copy_part.wait()
    s1[...] = (part[core] + part_far[...]).astype(BF16)

    def along_col(source, target, slot):
        def one(t, carry):
            c = (col + t) % 16
            pltpu.make_async_remote_copy(
                src_ref=source(c), dst_ref=target, send_sem=red_send.at[slot], recv_sem=red_recv.at[slot],
                device_id=(row, c), device_id_type=MESH,
            ).start()
            return carry

        lax.fori_loop(1, 16, one, 0)

    def all_of(view, semaphore):
        pltpu.make_async_copy(view, view, semaphore).wait()

    along_col(lambda c: s1.at[c], r1.at[col], 0)
    r1[col] = s1[col]
    all_of(r1.at[pl.ds(0, 15)], red_recv.at[0])
    s2[...] = jnp.sum(r1[...].astype(F32), axis=0).astype(BF16)

    def along_row(t, carry):
        r = (rx + t) % 8
        pltpu.make_async_remote_copy(
            src_ref=s2, dst_ref=r2.at[rx], send_sem=red_send.at[1], recv_sem=red_recv.at[1],
            device_id=(r * 2 + core, col), device_id_type=MESH,
        ).start()
        return carry

    lax.fori_loop(1, 8, along_row, 0)
    r2[rx] = s2[...]
    all_of(r2.at[pl.ds(0, 7)], red_recv.at[1])
    total = jnp.sum(r2[...].astype(F32), axis=0)
    gain_grad_o[...] = total[24:26]
    final[core, col] = total[0:24]
    along_col(lambda c: final.at[core, col], final.at[core, col], 2)
    all_of(final.at[core, pl.ds(0, 15)], red_recv.at[2])
    copy_final = to_sibling(final.at[core], final.at[core], 3)
    copy_final.start()
    copy_final.wait()
    first = final[0].reshape(384, 128)
    second = final[1].reshape(384, 128)
    for b in range(3):
        weight_grad_o[:, pl.ds(b * 128, 128)] = first[b * 128 : b * 128 + 128]
    for b in range(2):
        weight_grad_o[:, pl.ds(384 + b * 128, 128)] = second[b * 128 : b * 128 + 128]
    out_weight_grad_o[...] = second[256:384]

    arrive(sb1, send.at[0])
    arrive(rb2, send.at[1])
    arrive(sb3, send.at[2])
    arrive(rb4, send.at[3])
    all_of(r1.at[pl.ds(0, 15)], red_send.at[0])
    all_of(r2.at[pl.ds(0, 7)], red_send.at[1])
    all_of(final.at[core, pl.ds(0, 15)], red_send.at[2])


def on_device(pair, gain_in, in_weight, gain_out, out_weight, out_grad):
    vmem = pl.BlockSpec(memory_space=pltpu.VMEM)
    scratch = [
        ((128, 16, 128), F32),
        ((128, 16, 128), BF16),
        ((8, 4, 4, 16, 128), BF16),
        ((8, 4, 8, 512), F32),
        ((8, 4, 8, 512), F32),
        ((2, 2, 256, 512), BF16),
        ((2, 8, 2, 4, 8, 128), BF16),
        ((128, 8, 128), BF16),
        ((128, 8, 128), BF16),
        ((2, 8, 2, 4, 8, 128), BF16),
        ((2, 256, 256), BF16),
        ((256, 256), BF16),
        ((8, 4, 4, 16, 128), BF16),
        ((128, 16, 128), BF16),
        ((128, 1024), BF16),
        ((128, 1024), F32),
        ((1, 1024), F32),
        ((5, 128, 1024), F32),
        ((128, 1024), BF16),
        ((128, 1024), F32),
        ((128, 1024), F32),
        ((640, 1024), BF16),
        ((640, 128), BF16),
        ((128, 128), BF16),
        ((128, 128), F32),
        ((128, 128), F32),
        ((2, 16, 32, 128), F32),
        ((16, 32, 128), F32),
        ((16, 32, 128), BF16),
        ((16, 32, 128), BF16),
        ((32, 128), BF16),
        ((8, 32, 128), BF16),
        ((2, 16, 24, 128), F32),
    ]
    update, pair_grad, in_weight_grad, out_weight_grad, gain_grad = pl.pallas_call(
        kernel,
        out_shape=(
            jax.ShapeDtypeStruct((4, 8, 32, 128), BF16),
            jax.ShapeDtypeStruct((4, 8, 32, 128), F32),
            jax.ShapeDtypeStruct((128, 640), F32),
            jax.ShapeDtypeStruct((128, 128), F32),
            jax.ShapeDtypeStruct((2, 128), F32),
        ),
        in_specs=[vmem] * 6,
        out_specs=[vmem] * 5,
        scratch_shapes=[pltpu.VMEM(shape, kind) for shape, kind in scratch]
        + [pltpu.SemaphoreType.DMA((4,))] * 4
        + [pltpu.SemaphoreType.DMA((3,))] * 2,
        compiler_params=pltpu.CompilerParams(
            collective_id=0, has_side_effects=True, vmem_limit_bytes=48 * 2**20
        ),
    )(
        pair.reshape(4, 8, 32, 128), gain_in.reshape(1, 128), in_weight,
        gain_out.reshape(1, 128), out_weight, out_grad.reshape(4, 8, 32, 128),
    )
    return (
        update.reshape(32, 32, 128), pair_grad.reshape(32, 32, 128),
        in_weight_grad, out_weight_grad, gain_grad,
    )


def solution(mesh):
    return jax.shard_map(
        on_device,
        mesh=mesh,
        in_specs=(P("row", "col", None), P(), P(), P(), P(), P("row", "col", None)),
        out_specs=(P("row", "col", None), P("row", "col", None), P(), P(), P()),
        check_vma=False,
    )
```

time: 895 us -> 106 us (0.12)
  waiting for transfers between devices: 712 us -> 0 us
  Pallas kernels: 0 us -> 97.3 us
  blocking collectives: 79 us -> 0 us
  local copies, waits for them, and re-layouts: 42.6 us -> 7.64 us
  matrix products: 32.4 us -> 0 us
  between operations: 14 us -> 0.66 us
  other arithmetic: 13.2 us -> 0 us
    reduce_scatter x2 -> x0, waiting for transfers between devices: 274 us -> none  [the longest x1 219 us: on_device(): mixed = lax.psum_scatter(pair_term, 'col', scatter_dimension=1, tiled=True)]
    psum x1 -> x0, waiting for transfers between devices: 244 us -> none  [on_device(): lax.psum((in_weight_part, out_weight_part, jnp.stack([gain_in_part, gain_...]
    all_gather x2 -> x0, waiting for transfers between devices: 195 us -> none  [the longest x1 99.3 us: on_device(): grad_whole = lax.all_gather(grad_mixed_bf, 'col', axis=1, tiled=True)]
    pallas_call x0 -> x1, Pallas kernels: none -> 97.3 us  [on_device(): pl.pallas_call(kernel, out_shape=(jax.ShapeDtypeStruct((4, 8, 32, 128), B...]
    psum x1 -> x0, blocking collectives: 79 us -> none  [on_device(): lax.psum((in_weight_part, out_weight_part, jnp.stack([gain_in_part, gain_...]
    dot_general x9 -> x0, matrix products: 32.4 us -> none  [the longest x1 11.5 us: on_device(): jnp.einsum('ikc,jkc->ijc', left_bf, right_whole, preferred_element_type=j...]
    transpose x2 -> x0, local copies, waits for them, and re-layouts: 12.4 us -> none  [the longest x1 11 us: on_device(): jnp.einsum('ikc,jkc->ijc', left_bf, right_whole, preferred_element_type=j...]
    convert_element_type x1 -> x0, local copies, waits for them, and re-layouts: 9.13 us -> none  [on_device(): right_term.astype(jnp.bfloat16)]
  transfers between devices with their start and end apart: 5 -> 0, of which waited for: 5 -> 0; matrix products, arithmetic and copies ran while one was open for 2% -> 0% of each run, Pallas kernels for 0% -> 0%
where the time goes in v1:
time: 106 us
  Pallas kernels  97.3 us (92%)
  local copies, waits for them, and re-layouts  7.64 us (7%)
    pallas_call x1, Pallas kernels, on_device(): pl.pallas_call(kernel, out_shape=(jax.ShapeDtypeStruct((4, 8, 32, 128), B...  97.3 us
    unnamed x17, local copies, waits for them, and re-layouts  7.64 us

profile of v1, /device:TPU:1, one launch (start us, length us, event | category | flops | bytes accessed | tf_op | source)
XLA Modules:
  0.0 105.6 jit_solution(6804143288175836316)
XLA Ops:
  0.6 0.0 copy-start.4
  0.6 0.0 copy-start.5
  0.7 0.6 copy-done.4
  1.3 0.0 copy-done.5
  1.3 0.0 copy-start
  1.3 0.9 copy-done
  2.3 0.0 copy-start.1
  2.3 0.9 copy-done.1
  3.2 0.0 copy-start.2
  3.2 0.9 copy-done.2
  4.1 0.0 copy-start.3
  4.1 0.8 copy-done.3
  4.9 97.3 %shard_map.101 = (bf16[4,8,32,128]{3,2,1,0:T(8,128)(2,1)S(1)}, f32[4,8,32,128]{3,2,1,0:T(8,128)S(1)}, f32[128,640]{1,0:T(8,128)S(1)}, f32[128,128]{1,0:T(8,128)S(1)}, f32[2,128]{1,0:T(2,128)S(1)}) custom-call(bf16[4,8,32,128]{3,2,1,0:T(8,128)(2,1)S(1)} %bitcast.7, f32[1,128]{1,0:T(1,128)S(1)} %bitcast.10, bf16[128,640]{1,0:T(8,128)(2,1)S(1)} %copy-done.2, ...), custom_call_target="tpu_custom_call" | custom-call | tf_op jit(solution)/shard_map/pallas_call | solution.py:346
  102.2 0.7 copy.16
  102.9 0.8 copy.17
  103.7 0.7 copy.18
  104.4 0.6 copy.19
  105.0 0.6 copy.20
Async XLA Ops:
  0.6 0.7 copy-start.4
  0.6 0.7 copy-start.5
  1.3 0.9 copy-start
  2.3 0.9 copy-start.1
  3.2 0.9 copy-start.2
  4.1 0.8 copy-start.3

commit v2 on v1

v2 whole, which is shorter than its diff:
```python
import jax
import jax.numpy as jnp
from jax import lax
from jax.experimental import pallas as pl
from jax.experimental.pallas import tpu as pltpu
from jax.sharding import PartitionSpec as P

EPS = 1e-05
MESH = pl.DeviceIdType.MESH
F32 = jnp.float32
BF16 = jnp.bfloat16
NT = (((1,), (1,)), ((), ()))
TN = (((0,), (0,)), ((), ()))


def dot(a, b, dims=(((1,), (0,)), ((), ()))):
    return lax.dot_general(a, b, dims, preferred_element_type=F32)


def swap_blocks(tiles):
    shape = tiles[0].shape
    flat = [t.reshape(-1, 128) for t in tiles]
    lane = lax.broadcasted_iota(jnp.int32, flat[0].shape, 1)
    low = lane < 64
    even = (lane // 32) % 2 == 0
    half = [None] * 4
    for q in range(2):
        a, b = flat[q], flat[q + 2]
        half[q] = jnp.where(low, a, pltpu.roll(b, 64, 1))
        half[q + 2] = jnp.where(low, pltpu.roll(a, 64, 1), b)
    out = [None] * 4
    for q in (0, 2):
        a, b = half[q], half[q + 1]
        out[q] = jnp.where(even, a, pltpu.roll(b, 32, 1))
        out[q + 1] = jnp.where(even, pltpu.roll(a, 96, 1), b)
    return [t.reshape(shape) for t in out]


def kernel(
    pair_h, gain_in_h, weight_h, gain_out_h, out_weight_h, out_grad_h,
    update_o, pair_grad_o, weight_grad_o, out_weight_grad_o, gain_grad_o,
    pair, weight, out_weight, out_grad, gain_in, gain_out,
    wide, sb1, rb1, edges, sb2, rb2, sb3, rb3, grad_mat, grad_far, sb4, rb4,
    normed, hat_in, rstd_in, gates, grad_po, grad_no, og_t, grad_p, w_t, ow_t, g_in, g_out,
    sb5, rb5, sums, sums_far, total_bf, final,
    load, send, recv, sib_send, sib_recv,
):
    row, col = lax.axis_index("row"), lax.axis_index("col")
    core, rx = lax.rem(row, 2), lax.div(row, 2)
    me = rx * 16 + col
    sibling = (rx * 2 + 1 - core, col)
    barrier = pltpu.get_barrier_semaphore()

    def partners(act):
        def line(dr, first):
            r = lax.rem(rx + dr, 8)

            def one(dc, carry):
                act(dr, r, lax.rem(col + dc, 16))
                return carry

            lax.fori_loop(first, 16, one, 0, unroll=True)

        def rest(dr, carry):
            line(dr, 0)
            return carry

        line(0, 1)
        lax.fori_loop(1, 8, rest, 0)

    def greet(dr, r, c):
        pl.semaphore_signal(barrier, inc=1, device_id=(r * 2 + core, c), device_id_type=MESH)

    loads = [
        pltpu.make_async_copy(source, target, load.at[i])
        for i, (source, target) in enumerate(
            [
                (pair_h, pair), (weight_h, weight), (out_weight_h, out_weight), (out_grad_h, out_grad),
                (gain_in_h, gain_in), (gain_out_h, gain_out),
            ]
        )
    ]
    for copy in loads:
        copy.start()
    partners(greet)
    pl.semaphore_signal(barrier, inc=1, device_id=sibling, device_id_type=MESH)

    def exchange(source, target, slot):
        def one(dr, r, c):
            pltpu.make_async_remote_copy(
                src_ref=source.at[r * 16 + c], dst_ref=target.at[me], send_sem=send.at[slot],
                recv_sem=recv.at[slot, dr], device_id=(r * 2 + core, c), device_id_type=MESH,
            ).start()

        partners(one)
        target[me] = source[me]

    def drain(buffer, count, semaphore):
        view = buffer.at[pl.ds(0, count)]
        pltpu.make_async_copy(view, view, semaphore).wait()

    def arrive(buffer, slot):
        drain(buffer, 15, recv.at[slot, 0])

        def one(dr, carry):
            drain(buffer, 16, recv.at[slot, dr])
            return carry

        lax.fori_loop(1, 8, one, 0)

    def to_sibling(source, target, slot):
        return pltpu.make_async_remote_copy(
            src_ref=source, dst_ref=target, send_sem=sib_send.at[slot], recv_sem=sib_recv.at[slot],
            device_id=sibling, device_id_type=MESH,
        )

    loads[4].wait()
    loads[5].wait()
    g_in[...] = jnp.broadcast_to(gain_in[...], (128, 128)).T
    g_out[...] = jnp.broadcast_to(gain_out[...], (128, 128)).T
    loads[0].wait()
    loads[1].wait()
    w_t[...] = weight[...].astype(F32).T.astype(BF16)
    for s in range(8):
        lanes = pl.ds(s * 128, 128)
        x = pair[:, s].reshape(128, 128).astype(F32).T
        centred = x - jnp.mean(x, axis=0, keepdims=True)
        rstd = lax.rsqrt(jnp.mean(centred * centred, axis=0, keepdims=True) + EPS)
        hat = centred * rstd
        hat_in[:, lanes] = hat
        rstd_in[:, lanes] = rstd
        n = (hat * g_in[...]).astype(BF16)
        normed[:, lanes] = n
        p = dot(w_t[pl.ds(0, 512)], n)
        s0, p1 = jax.nn.sigmoid(p[0:128]), p[128:256]
        s2, p3 = jax.nn.sigmoid(p[256:384]), p[384:512]
        gates[0, :, lanes] = s0
        gates[1, :, lanes] = p1
        gates[2, :, lanes] = s2
        gates[3, :, lanes] = p3
        wide[:, s, :] = s0 * p1
        wide[:, 8 + s, :] = s2 * p3
    sb1[...] = wide[...].astype(BF16)

    pl.semaphore_wait(barrier, 128)
    exchange(sb1, rb1, 0)

    loads[2].wait()
    loads[3].wait()
    ow_t[...] = out_weight[...].astype(F32).T.astype(BF16)
    for s in range(8):
        lanes = pl.ds(s * 128, 128)
        gate = jax.nn.sigmoid(dot(w_t[pl.ds(512, 128)], normed[:, lanes]))
        gates[4, :, lanes] = gate
        cotangent = out_grad[:, s].reshape(128, 128).astype(F32).T
        og_t[:, lanes] = cotangent
        gpo = (cotangent * gate).astype(BF16)
        grad_po[:, lanes] = gpo
        grad_no[:, lanes] = dot(out_weight[...], gpo)

    def edge_rows(dr):
        r = lax.rem(rx + 8 - dr, 8)
        parts = []
        for g in range(4):
            parts.append(swap_blocks([rb1[r * 16 + 4 * g + q].astype(F32) for q in range(4)]))
        for side in range(2):
            rows = [
                jnp.concatenate([parts[g][a][8 * side : 8 * side + 8] for g in range(4)], axis=1)
                for a in range(4)
            ]
            edges[0, side, r] = jnp.concatenate(rows, axis=0).astype(BF16)
            to_sibling(edges.at[0, side, r], edges.at[1, side, r], side).start()

    drain(sb1, 15, recv.at[0, 0])
    edge_rows(0)

    def edge_group(dr, carry):
        drain(sb1, 16, recv.at[0, dr])
        edge_rows(dr)
        return carry

    lax.fori_loop(1, 8, edge_group, 0)

    def side_of(slot, side):
        return edges[slot, side].reshape(256, 512)

    def place(slot):
        return core if slot == 0 else 1 - core

    def send_mixed(slot):
        mixed = dot(side_of(0, 0), side_of(slot, 1), NT).reshape(8, 4, 8, 256)
        for g in range(2):
            tiles = swap_blocks([mixed[:, a, :, g * 128 : g * 128 + 128] for a in range(4)])
            for q in range(4):
                sb2.reshape(8, 16, 8, 128)[:, 2 * (4 * g + q) + place(slot)] = tiles[q].astype(BF16)

    send_mixed(0)
    to_sibling(edges.at[0, 1], edges.at[1, 1], 1).wait_recv()
    send_mixed(1)
    exchange(sb2, rb2, 1)
    arrive(rb2, 1)

    wide[:, 0:8, :] = rb2[...].astype(F32)
    gain_sum = jnp.zeros((128, 128), F32)
    for s in range(8):
        lanes = pl.ds(s * 128, 128)
        x = wide[:, s, :]
        centred = x - jnp.mean(x, axis=0, keepdims=True)
        rstd = lax.rsqrt(jnp.mean(centred * centred, axis=0, keepdims=True) + EPS)
        hat = centred * rstd
        gno = grad_no[:, lanes]
        gain_sum = gain_sum + gno * hat
        cot = gno * g_out[...]
        inner = jnp.mean(cot * hat, axis=0, keepdims=True)
        grad = rstd * (cot - jnp.mean(cot, axis=0, keepdims=True) - hat * inner)
        grad_no[:, lanes] = hat
        wide[:, 8 + s, :] = grad
    sb3[...] = wide[:, 8:16, :].astype(BF16)
    exchange(sb3, rb3, 2)

    gain_out_part = jnp.sum(gain_sum.T, axis=0, keepdims=True)
    for s in range(8):
        lanes = pl.ds(s * 128, 128)
        no = (grad_no[:, lanes] * g_out[...]).astype(BF16)
        grad_p[pl.ds(0, 128), lanes] = no
        po = dot(ow_t[...], no)
        gate = gates[4, :, lanes]
        update_o[:, s] = (gate * po).T.reshape(4, 32, 128).astype(BF16)
        grad_p[pl.ds(512, 128), lanes] = (og_t[:, lanes] * po * (gate * (1.0 - gate))).astype(BF16)

    def grad_rows(dr):
        r = lax.rem(rx + 8 - dr, 8)
        for slot in range(2):
            parts = []
            for g in range(2):
                parts.append(
                    swap_blocks([rb3[r * 16 + 2 * (4 * g + q) + place(slot)].astype(F32) for q in range(4)])
                )
            rows = [jnp.concatenate([parts[0][a], parts[1][a]], axis=1) for a in range(4)]
            grad_mat[slot, r] = jnp.concatenate(rows, axis=0).astype(BF16)
        to_sibling(grad_mat.at[1, r], grad_far.at[r], 2).start()

    drain(sb3, 15, recv.at[2, 0])
    grad_rows(0)

    def grad_group(dr, carry):
        drain(sb3, 16, recv.at[2, dr])
        grad_rows(dr)
        return carry

    lax.fori_loop(1, 8, grad_group, 0)
    to_sibling(edges.at[0, 0], edges.at[1, 0], 0).wait_recv()
    near, other = grad_mat[0].reshape(256, 256), grad_mat[1].reshape(256, 256)
    grad_left = (dot(near, side_of(0, 1)) + dot(other, side_of(1, 1))).reshape(8, 4, 8, 512)
    grad_right = dot(near, side_of(0, 0), TN)
    to_sibling(grad_mat.at[1], grad_far, 2).wait_recv()
    grad_right = (grad_right + dot(grad_far[...].reshape(256, 256), side_of(1, 0), TN)).reshape(8, 4, 8, 512)
    for g in range(4):
        lanes = slice(g * 128, g * 128 + 128)
        tiles = swap_blocks(
            [jnp.concatenate([grad_left[:, a, :, lanes], grad_right[:, a, :, lanes]], axis=1) for a in range(4)]
        )
        for q in range(4):
            sb4.reshape(8, 16, 16, 128)[:, 4 * g + q] = tiles[q].astype(BF16)
    exchange(sb4, rb4, 3)

    out_part = dot(grad_p[pl.ds(0, 128)], grad_po[...], NT)
    gate_part = dot(normed[...], grad_p[pl.ds(512, 128)], NT)
    sums[:, 4, :] = gate_part
    sums[:, 5, :] = out_part
    sums[:, 7, :] = jnp.broadcast_to(gain_out_part, (128, 128))

    arrive(rb4, 3)
    wide[...] = rb4[...].astype(F32)
    gain_sum = jnp.zeros((128, 128), F32)
    for s in range(8):
        lanes = pl.ds(s * 128, 128)
        gl, gr = wide[:, s, :], wide[:, 8 + s, :]
        s0, p1 = gates[0, :, lanes], gates[1, :, lanes]
        s2, p3 = gates[2, :, lanes], gates[3, :, lanes]
        dl, dr = gl * s0, gr * s2
        grad_p[pl.ds(0, 128), lanes] = (dl * p1 * (1.0 - s0)).astype(BF16)
        grad_p[pl.ds(128, 128), lanes] = dl.astype(BF16)
        grad_p[pl.ds(256, 128), lanes] = (dr * p3 * (1.0 - s2)).astype(BF16)
        grad_p[pl.ds(384, 128), lanes] = dr.astype(BF16)
        gni = dot(weight[...], grad_p[:, lanes])
        gain_sum = gain_sum + gni * hat_in[:, lanes]
        og_t[:, lanes] = gni
    gain_in_part = jnp.sum(gain_sum.T, axis=0, keepdims=True)
    in_part = dot(normed[...], grad_p[pl.ds(0, 512)], NT)
    for b in range(4):
        sums[:, b, :] = in_part[:, b * 128 : b * 128 + 128]
    sums[:, 6, :] = jnp.broadcast_to(gain_in_part, (128, 128))

    sb5[...] = sums[...].astype(BF16)
    exchange(sb5, rb5, 4)
    for s in range(8):
        lanes = pl.ds(s * 128, 128)
        hat = hat_in[:, lanes]
        cot = og_t[:, lanes] * g_in[...]
        inner = jnp.mean(cot * hat, axis=0, keepdims=True)
        grad = rstd_in[:, lanes] * (cot - jnp.mean(cot, axis=0, keepdims=True) - hat * inner)
        pair_grad_o[:, s] = grad.T.reshape(4, 32, 128)
    arrive(rb5, 4)
    sums[0] = jnp.sum(rb5[...].astype(F32), axis=0)
    copy_sums = to_sibling(sums.at[0], sums_far, 3)
    copy_sums.start()
    copy_sums.wait()
    total = sums[0] + sums_far[...]
    gain_grad_o[...] = total[6:8]
    total_bf[...] = total.astype(BF16)
    final[me] = total_bf[...]

    def gather(dr, r, c):
        pltpu.make_async_remote_copy(
            src_ref=total_bf, dst_ref=final.at[me], send_sem=send.at[5], recv_sem=recv.at[5, dr],
            device_id=(r * 2 + core, c), device_id_type=MESH,
        ).start()

    partners(gather)
    drain(sb1, 127, send.at[0])
    drain(rb2, 127, send.at[1])
    drain(sb3, 127, send.at[2])
    drain(rb4, 127, send.at[3])
    drain(sb5, 127, send.at[4])
    for side in range(2):
        to_sibling(edges.at[0, side], edges.at[1, side], side).wait_send()
    to_sibling(grad_mat.at[1], grad_far, 2).wait_send()
    arrive(rb5, 5)
    sums[...] = final[...].astype(F32)
    for b in range(5):
        weight_grad_o[:, pl.ds(b * 128, 128)] = sums[:, b, :]
    out_weight_grad_o[...] = sums[:, 5, :]
    drain(rb5, 127, send.at[5])


def write_out(*refs):
    count = len(refs) // 2
    copies = [
        pltpu.make_async_copy(refs[i], refs[count + i], refs[-1].at[i]) for i in range(count)
    ]
    for copy in copies:
        copy.start()
    for copy in copies:
        copy.wait()


def on_device(pair, gain_in, in_weight, gain_out, out_weight, out_grad):
    vmem = pl.BlockSpec(memory_space=pltpu.VMEM)
    hbm = pl.BlockSpec(memory_space=pltpu.HBM)
    scratch = [
        ((4, 8, 32, 128), BF16),
        ((128, 640), BF16),
        ((128, 128), BF16),
        ((4, 8, 32, 128), BF16),
        ((1, 128), F32),
        ((1, 128), F32),
        ((128, 16, 128), F32),
        ((128, 16, 128), BF16),
        ((128, 16, 128), BF16),
        ((2, 2, 8, 32, 512), BF16),
        ((128, 8, 128), BF16),
        ((128, 8, 128), BF16),
        ((128, 8, 128), BF16),
        ((128, 8, 128), BF16),
        ((2, 8, 32, 256), BF16),
        ((8, 32, 256), BF16),
        ((128, 16, 128), BF16),
        ((128, 16, 128), BF16),
        ((128, 1024), BF16),
        ((128, 1024), F32),
        ((1, 1024), F32),
        ((5, 128, 1024), F32),
        ((128, 1024), BF16),
        ((128, 1024), F32),
        ((128, 1024), F32),
        ((640, 1024), BF16),
        ((640, 128), BF16),
        ((128, 128), BF16),
        ((128, 128), F32),
        ((128, 128), F32),
        ((128, 8, 128), BF16),
        ((128, 8, 128), BF16),
        ((128, 8, 128), F32),
        ((8, 128), F32),
        ((8, 128), BF16),
        ((128, 8, 128), BF16),
    ]
    shapes = (
        jax.ShapeDtypeStruct((4, 8, 32, 128), BF16),
        jax.ShapeDtypeStruct((4, 8, 32, 128), F32),
        jax.ShapeDtypeStruct((128, 640), F32),
        jax.ShapeDtypeStruct((128, 128), F32),
        jax.ShapeDtypeStruct((2, 128), F32),
    )
    operands = [
        pltpu.with_memory_space_constraint(value, pltpu.HBM)
        for value in (
            pair.reshape(4, 8, 32, 128), gain_in.reshape(1, 128), in_weight,
            gain_out.reshape(1, 128), out_weight, out_grad.reshape(4, 8, 32, 128),
        )
    ]
    results = pl.pallas_call(
        kernel,
        out_shape=shapes,
        in_specs=[hbm] * 6,
        out_specs=[vmem] * 5,
        scratch_shapes=[pltpu.VMEM(shape, kind) for shape, kind in scratch]
        + [
            pltpu.SemaphoreType.DMA((6,)),
            pltpu.SemaphoreType.DMA((6,)),
            pltpu.SemaphoreType.DMA((6, 8)),
            pltpu.SemaphoreType.DMA((4,)),
            pltpu.SemaphoreType.DMA((4,)),
        ],
        compiler_params=pltpu.CompilerParams(
            collective_id=0, has_side_effects=True, vmem_limit_bytes=48 * 2**20
        ),
    )(*operands)
    update, pair_grad, in_weight_grad, out_weight_grad, gain_grad = pl.pallas_call(
        write_out,
        out_shape=shapes,
        in_specs=[vmem] * 5,
        out_specs=[hbm] * 5,
        scratch_shapes=[pltpu.SemaphoreType.DMA((5,))],
        compiler_params=pltpu.CompilerParams(vmem_limit_bytes=16 * 2**20),
    )(*results)
    return (
        update.reshape(32, 32, 128), pair_grad.reshape(32, 32, 128),
        in_weight_grad, out_weight_grad, gain_grad,
    )


def solution(mesh):
    return jax.shard_map(
        on_device,
        mesh=mesh,
        in_specs=(P("row", "col", None), P(), P(), P(), P(), P("row", "col", None)),
        out_specs=(P("row", "col", None), P("row", "col", None), P(), P(), P()),
        check_vma=False,
    )
```

time: 106 us -> 98 us (0.925)
  local copies, waits for them, and re-layouts: 7.64 us -> 0 us
    unnamed x17 -> x0, local copies, waits for them, and re-layouts: 7.64 us -> none
    pallas_call x1 -> x2, Pallas kernels: 97.3 us -> 97.3 us  [the longest x1 96.2 us: on_device(): pl.pallas_call(kernel, out_shape=shapes, in_specs=[hbm] * 6, out_specs=[v...]
where the time goes in v2:
time: 98 us; the launch traced here: 97.9 us
  Pallas kernels  97.3 us (99%)
    pallas_call x1, Pallas kernels, on_device(): pl.pallas_call(kernel, out_shape=shapes, in_specs=[hbm] * 6, out_specs=[v...  96.2 us

profile of v2, /device:TPU:1, one launch (start us, length us, event | category | flops | bytes accessed | tf_op | source)
XLA Modules:
  0.0 97.9 jit_solution(15417031324136058941)
XLA Ops:
  0.6 96.2 %shard_map.101 = (bf16[4,8,32,128]{3,2,1,0:T(8,128)(2,1)S(1)}, f32[4,8,32,128]{3,2,1,0:T(8,128)S(1)}, f32[128,640]{1,0:T(8,128)S(1)}, f32[128,128]{1,0:T(8,128)S(1)}, f32[2,128]{1,0:T(2,128)S(1)}) custom-call(bf16[4,8,32,128]{3,2,1,0:T(8,128)(2,1)} %bitcast.6, f32[1,128]{1,0:T(1,128)} %bitcast.8, bf16[128,640]{1,0:T(8,128)(2,1)} %weight_h.1, ...), custom_call_target="tpu_custom_call" | custom-call | tf_op jit(solution)/shard_map/pallas_call | solution.py:403
  96.9 1.0 %shard_map.102 = (bf16[4,8,32,128]{3,2,1,0:T(8,128)(2,1)}, f32[4,8,32,128]{3,2,1,0:T(8,128)}, f32[128,640]{1,0:T(8,128)}, f32[128,128]{1,0:T(8,128)}, f32[2,128]{1,0:T(2,128)}) custom-call(bf16[4,8,32,128]{3,2,1,0:T(8,128)(2,1)S(1)} %get-tuple-element.15.refs_0_, f32[4,8,32,128]{3,2,1,0:T(8,128)S(1)} %get-tuple-element.16.refs_1_, ...), custom_call_target="tpu_custom_call" | custom-call | tf_op jit(solution)/shard_map/pallas_call | solution.py:420

commit v3 on v2

--- a/solution.py
+++ b/solution.py
@@ -42,12 +42,14 @@
     pair, weight, out_weight, out_grad, gain_in, gain_out,
     wide, sb1, rb1, edges, sb2, rb2, sb3, rb3, grad_mat, grad_far, sb4, rb4,
     normed, hat_in, rstd_in, gates, grad_po, grad_no, og_t, grad_p, w_t, ow_t, g_in, g_out,
-    sb5, rb5, sums, sums_far, total_bf, final,
+    sb5, rb5, sums, plane_sum, planes, total_bf, final,
     load, send, recv, sib_send, sib_recv,
 ):
     row, col = lax.axis_index("row"), lax.axis_index("col")
     core, rx = lax.rem(row, 2), lax.div(row, 2)
     me = rx * 16 + col
+    half, z = lax.div(col, 2), lax.rem(col, 8)
+    spot = lax.div(col, 8) * 16 + row
     sibling = (rx * 2 + 1 - core, col)
     barrier = pltpu.get_barrier_semaphore()
 
@@ -83,7 +85,16 @@
     for copy in loads:
         copy.start()
     partners(greet)
-    pl.semaphore_signal(barrier, inc=1, device_id=sibling, device_id_type=MESH)
+
+    def in_plane(d):
+        p = lax.rem(spot + d, 32)
+        return p, (lax.rem(p, 16), lax.div(p, 16) * 8 + z)
+
+    def greet_plane(d, carry):
+        pl.semaphore_signal(barrier, inc=1, device_id=in_plane(2 * d + 1)[1], device_id_type=MESH)
+        return carry
+
+    lax.fori_loop(0, 16, greet_plane, 0, unroll=True)
 
     def exchange(source, target, slot):
         def one(dr, r, c):
@@ -142,7 +153,7 @@
         wide[:, 8 + s, :] = s2 * p3
     sb1[...] = wide[...].astype(BF16)
 
-    pl.semaphore_wait(barrier, 128)
+    pl.semaphore_wait(barrier, 143)
     exchange(sb1, rb1, 0)
 
     loads[2].wait()
@@ -194,10 +205,42 @@
             for q in range(4):
                 sb2.reshape(8, 16, 8, 128)[:, 2 * (4 * g + q) + place(slot)] = tiles[q].astype(BF16)
 
+    def exchange_mixed(slot):
+        parity = place(slot)
+
+        def start(dr, r, c):
+            pltpu.make_async_remote_copy(
+                src_ref=sb2.at[r * 16 + c], dst_ref=rb2.at[me], send_sem=send.at[1], recv_sem=recv.at[1, dr],
+                device_id=(r * 2 + core, c), device_id_type=MESH,
+            ).start()
+
+        def line(dr, first):
+            r = lax.rem(rx + dr, 8)
+
+            def one(k, carry):
+                start(dr, r, 2 * lax.rem(half + k, 8) + parity)
+                return carry
+
+            lax.fori_loop(first, 8, one, 0, unroll=True)
+
+        def rest(dr, carry):
+            line(dr, 0)
+            return carry
+
+        line(0, 1)
+
+        @pl.when(parity != lax.rem(col, 2))
+        def _():
+            start(0, rx, 2 * half + parity)
+
+        lax.fori_loop(1, 8, rest, 0)
+
     send_mixed(0)
+    exchange_mixed(0)
     to_sibling(edges.at[0, 1], edges.at[1, 1], 1).wait_recv()
     send_mixed(1)
-    exchange(sb2, rb2, 1)
+    exchange_mixed(1)
+    rb2[me] = sb2[me]
     arrive(rb2, 1)
 
     wide[:, 0:8, :] = rb2[...].astype(F32)
@@ -270,19 +313,32 @@
     sums[:, 5, :] = out_part
     sums[:, 7, :] = jnp.broadcast_to(gain_out_part, (128, 128))
 
-    arrive(rb4, 3)
-    wide[...] = rb4[...].astype(F32)
+    def edge_grads(dr):
+        first = pl.multiple_of(lax.rem(rx + 8 - dr, 8) * 16, 16)
+        here = pl.ds(first, 16)
+        wide[here] = rb4[here].astype(F32)
+        for s in range(8):
+            lanes = pl.ds(s * 128, 128)
+            gl, gr = wide[here, s, :], wide[here, 8 + s, :]
+            s0, p1 = gates[0, here, lanes], gates[1, here, lanes]
+            s2, p3 = gates[2, here, lanes], gates[3, here, lanes]
+            dl, dr_ = gl * s0, gr * s2
+            grad_p[here, lanes] = (dl * p1 * (1.0 - s0)).astype(BF16)
+            grad_p[pl.ds(128 + first, 16), lanes] = dl.astype(BF16)
+            grad_p[pl.ds(256 + first, 16), lanes] = (dr_ * p3 * (1.0 - s2)).astype(BF16)
+            grad_p[pl.ds(384 + first, 16), lanes] = dr_.astype(BF16)
+
+    def edge_grad_group(dr, carry):
+        drain(rb4, 16, recv.at[3, dr])
+        edge_grads(dr)
+        return carry
+
+    drain(rb4, 15, recv.at[3, 0])
+    edge_grads(0)
+    lax.fori_loop(1, 8, edge_grad_group, 0)
     gain_sum = jnp.zeros((128, 128), F32)
     for s in range(8):
         lanes = pl.ds(s * 128, 128)
-        gl, gr = wide[:, s, :], wide[:, 8 + s, :]
-        s0, p1 = gates[0, :, lanes], gates[1, :, lanes]
-        s2, p3 = gates[2, :, lanes], gates[3, :, lanes]
-        dl, dr = gl * s0, gr * s2
-        grad_p[pl.ds(0, 128), lanes] = (dl * p1 * (1.0 - s0)).astype(BF16)
-        grad_p[pl.ds(128, 128), lanes] = dl.astype(BF16)
-        grad_p[pl.ds(256, 128), lanes] = (dr * p3 * (1.0 - s2)).astype(BF16)
-        grad_p[pl.ds(384, 128), lanes] = dr.astype(BF16)
         gni = dot(weight[...], grad_p[:, lanes])
         gain_sum = gain_sum + gni * hat_in[:, lanes]
         og_t[:, lanes] = gni
@@ -292,8 +348,23 @@
         sums[:, b, :] = in_part[:, b * 128 : b * 128 + 128]
     sums[:, 6, :] = jnp.broadcast_to(gain_in_part, (128, 128))
 
+    def along_plane(source, target, slot):
+        def one(d, carry):
+            p, device = in_plane(d)
+            pltpu.make_async_remote_copy(
+                src_ref=source(p), dst_ref=target, send_sem=send.at[slot], recv_sem=recv.at[slot, 0],
+                device_id=device, device_id_type=MESH,
+            ).start()
+            return carry
+
+        lax.fori_loop(1, 32, one, 0, unroll=True)
+
+    def rows_of(p):
+        return pl.ds(pl.multiple_of(p * 4, 4), 4)
+
     sb5[...] = sums[...].astype(BF16)
-    exchange(sb5, rb5, 4)
+    along_plane(lambda p: sb5.at[rows_of(p)], rb5.at[spot], 4)
+    rb5[spot] = sb5[rows_of(spot)]
     for s in range(8):
         lanes = pl.ds(s * 128, 128)
         hat = hat_in[:, lanes]
@@ -301,37 +372,39 @@
         inner = jnp.mean(cot * hat, axis=0, keepdims=True)
         grad = rstd_in[:, lanes] * (cot - jnp.mean(cot, axis=0, keepdims=True) - hat * inner)
         pair_grad_o[:, s] = grad.T.reshape(4, 32, 128)
-    arrive(rb5, 4)
-    sums[0] = jnp.sum(rb5[...].astype(F32), axis=0)
-    copy_sums = to_sibling(sums.at[0], sums_far, 3)
-    copy_sums.start()
-    copy_sums.wait()
-    total = sums[0] + sums_far[...]
-    gain_grad_o[...] = total[6:8]
+    drain(rb5, 31, recv.at[4, 0])
+    plane_sum[...] = jnp.sum(rb5[...].astype(F32), axis=0).astype(BF16)
+
+    def along_z(d, carry):
+        pltpu.make_async_remote_copy(
+            src_ref=plane_sum, dst_ref=planes.at[z], send_sem=send.at[5], recv_sem=recv.at[5, 0],
+            device_id=(row, lax.div(col, 8) * 8 + lax.rem(z + d, 8)), device_id_type=MESH,
+        ).start()
+        return carry
+
+    lax.fori_loop(1, 8, along_z, 0, unroll=True)
+    planes[z] = plane_sum[...]
+    drain(planes, 7, recv.at[5, 0])
+    total = jnp.sum(planes[...].astype(F32), axis=0)
+    gain_grad_o[...] = total[0, 6:8]
     total_bf[...] = total.astype(BF16)
-    final[me] = total_bf[...]
-
-    def gather(dr, r, c):
-        pltpu.make_async_remote_copy(
-            src_ref=total_bf, dst_ref=final.at[me], send_sem=send.at[5], recv_sem=recv.at[5, dr],
-            device_id=(r * 2 + core, c), device_id_type=MESH,
-        ).start()
-
-    partners(gather)
+    along_plane(lambda p: total_bf, final.at[rows_of(spot)], 6)
+    final[rows_of(spot)] = total_bf[...]
     drain(sb1, 127, send.at[0])
     drain(rb2, 127, send.at[1])
     drain(sb3, 127, send.at[2])
     drain(rb4, 127, send.at[3])
-    drain(sb5, 127, send.at[4])
+    drain(rb5, 31, send.at[4])
+    drain(planes, 7, send.at[5])
+    drain(rb5, 31, send.at[6])
     for side in range(2):
         to_sibling(edges.at[0, side], edges.at[1, side], side).wait_send()
     to_sibling(grad_mat.at[1], grad_far, 2).wait_send()
-    arrive(rb5, 5)
+    drain(rb5, 31, recv.at[6, 0])
     sums[...] = final[...].astype(F32)
     for b in range(5):
         weight_grad_o[:, pl.ds(b * 128, 128)] = sums[:, b, :]
     out_weight_grad_o[...] = sums[:, 5, :]
-    drain(rb5, 127, send.at[5])
 
 
 def write_out(*refs):
@@ -380,10 +453,11 @@
         ((128, 128), F32),
         ((128, 128), F32),
         ((128, 8, 128), BF16),
-        ((128, 8, 128), BF16),
+        ((32, 4, 8, 128), BF16),
         ((128, 8, 128), F32),
-        ((8, 128), F32),
-        ((8, 128), BF16),
+        ((4, 8, 128), BF16),
+        ((8, 4, 8, 128), BF16),
+        ((4, 8, 128), BF16),
         ((128, 8, 128), BF16),
     ]
     shapes = (
@@ -408,10 +482,10 @@
         scratch_shapes=[pltpu.VMEM(shape, kind) for shape, kind in scratch]
         + [
             pltpu.SemaphoreType.DMA((6,)),
-            pltpu.SemaphoreType.DMA((6,)),
-            pltpu.SemaphoreType.DMA((6, 8)),
-            pltpu.SemaphoreType.DMA((4,)),
-            pltpu.SemaphoreType.DMA((4,)),
+            pltpu.SemaphoreType.DMA((7,)),
+            pltpu.SemaphoreType.DMA((7, 8)),
+            pltpu.SemaphoreType.DMA((3,)),
+            pltpu.SemaphoreType.DMA((3,)),
         ],
         compiler_params=pltpu.CompilerParams(
             collective_id=0, has_side_effects=True, vmem_limit_bytes=48 * 2**20

time: 98 us -> 88.1 us (0.90)
  Pallas kernels: 97.3 us -> 87.4 us
    pallas_call x1, Pallas kernels: 96.2 us -> 86.3 us  [on_device(): pl.pallas_call(kernel, out_shape=shapes, in_specs=[hbm] * 6, out_specs=[v...]
where the time goes in v3:
time: 88.1 us; the launch traced here: 88 us
  Pallas kernels  87.4 us (99%)
    pallas_call x1, Pallas kernels, on_device(): pl.pallas_call(kernel, out_shape=shapes, in_specs=[hbm] * 6, out_specs=[v...  86.3 us

profile of v3, /device:TPU:1, one launch (start us, length us, event | category | flops | bytes accessed | tf_op | source)
XLA Modules:
  0.0 88.0 jit_solution(17252030478416920117)
XLA Ops:
  0.6 86.3 %shard_map.101 = (bf16[4,8,32,128]{3,2,1,0:T(8,128)(2,1)S(1)}, f32[4,8,32,128]{3,2,1,0:T(8,128)S(1)}, f32[128,640]{1,0:T(8,128)S(1)}, f32[128,128]{1,0:T(8,128)S(1)}, f32[2,128]{1,0:T(2,128)S(1)}) custom-call(bf16[4,8,32,128]{3,2,1,0:T(8,128)(2,1)} %bitcast.6, f32[1,128]{1,0:T(1,128)} %bitcast.8, bf16[128,640]{1,0:T(8,128)(2,1)} %weight_h.1, ...), custom_call_target="tpu_custom_call" | custom-call | tf_op jit(solution)/shard_map/pallas_call | solution.py:477
  87.0 1.0 %shard_map.102 = (bf16[4,8,32,128]{3,2,1,0:T(8,128)(2,1)}, f32[4,8,32,128]{3,2,1,0:T(8,128)}, f32[128,640]{1,0:T(8,128)}, f32[128,128]{1,0:T(8,128)}, f32[2,128]{1,0:T(2,128)}) custom-call(bf16[4,8,32,128]{3,2,1,0:T(8,128)(2,1)S(1)} %get-tuple-element.15.refs_0_, f32[4,8,32,128]{3,2,1,0:T(8,128)S(1)} %get-tuple-element.16.refs_1_, ...), custom_call_target="tpu_custom_call" | custom-call | tf_op jit(solution)/shard_map/pallas_call | solution.py:494

commit v4 on v3

--- a/solution.py
+++ b/solution.py
@@ -40,7 +40,7 @@
     pair_h, gain_in_h, weight_h, gain_out_h, out_weight_h, out_grad_h,
     update_o, pair_grad_o, weight_grad_o, out_weight_grad_o, gain_grad_o,
     pair, weight, out_weight, out_grad, gain_in, gain_out,
-    wide, sb1, rb1, edges, sb2, rb2, sb3, rb3, grad_mat, grad_far, sb4, rb4,
+    wide, sb0, rb0, sb1, rb1, edges, sb2, rb2, sb3, rb3, grad_mat, grad_far, sb4, rb4, sb6, rb6,
     normed, hat_in, rstd_in, gates, grad_po, grad_no, og_t, grad_p, w_t, ow_t, g_in, g_out,
     sb5, rb5, sums, plane_sum, planes, total_bf, final,
     load, send, recv, sib_send, sib_recv,
@@ -48,7 +48,7 @@
     row, col = lax.axis_index("row"), lax.axis_index("col")
     core, rx = lax.rem(row, 2), lax.div(row, 2)
     me = rx * 16 + col
-    half, z = lax.div(col, 2), lax.rem(col, 8)
+    z = lax.rem(col, 8)
     spot = lax.div(col, 8) * 16 + row
     sibling = (rx * 2 + 1 - core, col)
     barrier = pltpu.get_barrier_semaphore()
@@ -109,6 +109,17 @@
     def drain(buffer, count, semaphore):
         view = buffer.at[pl.ds(0, count)]
         pltpu.make_async_copy(view, view, semaphore).wait()
+
+    def send_row(source, target, slot, dr, r, first):
+        def one(dc, carry):
+            c = lax.rem(col + dc, 16)
+            pltpu.make_async_remote_copy(
+                src_ref=source.at[r * 16 + c], dst_ref=target.at[me], send_sem=send.at[slot],
+                recv_sem=recv.at[slot, dr], device_id=(r * 2 + core, c), device_id_type=MESH,
+            ).start()
+            return carry
+
+        lax.fori_loop(first, 16, one, 0, unroll=True)
 
     def arrive(buffer, slot):
         drain(buffer, 15, recv.at[slot, 0])
@@ -151,10 +162,12 @@
         gates[3, :, lanes] = p3
         wide[:, s, :] = s0 * p1
         wide[:, 8 + s, :] = s2 * p3
-    sb1[...] = wide[...].astype(BF16)
+    sb1[...] = wide[:, 8:16, :].astype(BF16)
+    sb0[...] = wide[:, 0:8, :].astype(BF16)
 
     pl.semaphore_wait(barrier, 143)
     exchange(sb1, rb1, 0)
+    exchange(sb0, rb0, 8)
 
     loads[2].wait()
     loads[3].wait()
@@ -169,78 +182,49 @@
         grad_po[:, lanes] = gpo
         grad_no[:, lanes] = dot(out_weight[...], gpo)
 
-    def edge_rows(dr):
-        r = lax.rem(rx + 8 - dr, 8)
+    def side_of(slot, side):
+        return edges[slot, side].reshape(256, 512)
+
+    def place(slot):
+        return core if slot == 0 else 1 - core
+
+    def edge_rows(buffer, side, r):
         parts = []
         for g in range(4):
-            parts.append(swap_blocks([rb1[r * 16 + 4 * g + q].astype(F32) for q in range(4)]))
-        for side in range(2):
-            rows = [
-                jnp.concatenate([parts[g][a][8 * side : 8 * side + 8] for g in range(4)], axis=1)
-                for a in range(4)
-            ]
-            edges[0, side, r] = jnp.concatenate(rows, axis=0).astype(BF16)
-            to_sibling(edges.at[0, side, r], edges.at[1, side, r], side).start()
-
-    drain(sb1, 15, recv.at[0, 0])
-    edge_rows(0)
-
-    def edge_group(dr, carry):
-        drain(sb1, 16, recv.at[0, dr])
-        edge_rows(dr)
-        return carry
-
-    lax.fori_loop(1, 8, edge_group, 0)
-
-    def side_of(slot, side):
-        return edges[slot, side].reshape(256, 512)
-
-    def place(slot):
-        return core if slot == 0 else 1 - core
-
-    def send_mixed(slot):
-        mixed = dot(side_of(0, 0), side_of(slot, 1), NT).reshape(8, 4, 8, 256)
-        for g in range(2):
-            tiles = swap_blocks([mixed[:, a, :, g * 128 : g * 128 + 128] for a in range(4)])
-            for q in range(4):
-                sb2.reshape(8, 16, 8, 128)[:, 2 * (4 * g + q) + place(slot)] = tiles[q].astype(BF16)
-
-    def exchange_mixed(slot):
-        parity = place(slot)
-
-        def start(dr, r, c):
-            pltpu.make_async_remote_copy(
-                src_ref=sb2.at[r * 16 + c], dst_ref=rb2.at[me], send_sem=send.at[1], recv_sem=recv.at[1, dr],
-                device_id=(r * 2 + core, c), device_id_type=MESH,
-            ).start()
-
-        def line(dr, first):
-            r = lax.rem(rx + dr, 8)
-
-            def one(k, carry):
-                start(dr, r, 2 * lax.rem(half + k, 8) + parity)
-                return carry
-
-            lax.fori_loop(first, 8, one, 0, unroll=True)
-
-        def rest(dr, carry):
-            line(dr, 0)
-            return carry
-
-        line(0, 1)
-
-        @pl.when(parity != lax.rem(col, 2))
-        def _():
-            start(0, rx, 2 * half + parity)
-
-        lax.fori_loop(1, 8, rest, 0)
-
-    send_mixed(0)
-    exchange_mixed(0)
+            parts.append(swap_blocks([buffer[r * 16 + 4 * g + q].astype(F32) for q in range(4)]))
+        rows = [jnp.concatenate([parts[g][a] for g in range(4)], axis=1) for a in range(4)]
+        edges[0, side, r] = jnp.concatenate(rows, axis=0).astype(BF16)
+        to_sibling(edges.at[0, side, r], edges.at[1, side, r], side).start()
+
+    def right_group(dr, carry):
+        drain(rb1, 16, recv.at[0, dr])
+        edge_rows(rb1, 1, lax.rem(rx + 8 - dr, 8))
+        return carry
+
+    drain(rb1, 15, recv.at[0, 0])
+    edge_rows(rb1, 1, rx)
+    lax.fori_loop(1, 8, right_group, 0)
     to_sibling(edges.at[0, 1], edges.at[1, 1], 1).wait_recv()
-    send_mixed(1)
-    exchange_mixed(1)
+
+    def send_mixed(dr, r, first):
+        edge_rows(rb0, 0, r)
+        for slot in range(2):
+            rows = dot(edges[0, 0, r], side_of(slot, 1), NT)
+            for g in range(2):
+                tiles = swap_blocks([rows[8 * a : 8 * a + 8, g * 128 : g * 128 + 128] for a in range(4)])
+                for q in range(4):
+                    sb2[r * 16 + 2 * (4 * g + q) + place(slot)] = tiles[q].astype(BF16)
+        send_row(sb2, rb2, 1, dr, r, first)
+
+    def mixed_group(dr, carry):
+        drain(rb0, 16, recv.at[8, dr])
+        send_mixed(dr, lax.rem(rx + 8 - dr, 8), 0)
+        return carry
+
+    drain(rb0, 15, recv.at[8, 0])
+    send_mixed(0, rx, 1)
     rb2[me] = sb2[me]
+    lax.fori_loop(1, 8, mixed_group, 0)
     arrive(rb2, 1)
 
     wide[:, 0:8, :] = rb2[...].astype(F32)
@@ -283,29 +267,38 @@
             grad_mat[slot, r] = jnp.concatenate(rows, axis=0).astype(BF16)
         to_sibling(grad_mat.at[1, r], grad_far.at[r], 2).start()
 
+    def send_left(dr, first):
+        r = lax.rem(rx + 8 - dr, 8)
+        rows = dot(grad_mat[0, r], side_of(0, 1)) + dot(grad_mat[1, r], side_of(1, 1))
+        for g in range(4):
+            tiles = swap_blocks([rows[8 * a : 8 * a + 8, g * 128 : g * 128 + 128] for a in range(4)])
+            for q in range(4):
+                sb4[r * 16 + 4 * g + q] = tiles[q].astype(BF16)
+
+        send_row(sb4, rb4, 3, dr, r, first)
+
     drain(sb3, 15, recv.at[2, 0])
     grad_rows(0)
+    send_left(0, 1)
+    rb4[me] = sb4[me]
 
     def grad_group(dr, carry):
         drain(sb3, 16, recv.at[2, dr])
         grad_rows(dr)
+        send_left(dr, 0)
         return carry
 
     lax.fori_loop(1, 8, grad_group, 0)
     to_sibling(edges.at[0, 0], edges.at[1, 0], 0).wait_recv()
-    near, other = grad_mat[0].reshape(256, 256), grad_mat[1].reshape(256, 256)
-    grad_left = (dot(near, side_of(0, 1)) + dot(other, side_of(1, 1))).reshape(8, 4, 8, 512)
+    near = grad_mat[0].reshape(256, 256)
     grad_right = dot(near, side_of(0, 0), TN)
     to_sibling(grad_mat.at[1], grad_far, 2).wait_recv()
     grad_right = (grad_right + dot(grad_far[...].reshape(256, 256), side_of(1, 0), TN)).reshape(8, 4, 8, 512)
     for g in range(4):
-        lanes = slice(g * 128, g * 128 + 128)
-        tiles = swap_blocks(
-            [jnp.concatenate([grad_left[:, a, :, lanes], grad_right[:, a, :, lanes]], axis=1) for a in range(4)]
-        )
+        tiles = swap_blocks([grad_right[:, a, :, g * 128 : g * 128 + 128] for a in range(4)])
         for q in range(4):
-            sb4.reshape(8, 16, 16, 128)[:, 4 * g + q] = tiles[q].astype(BF16)
-    exchange(sb4, rb4, 3)
+            sb6.reshape(8, 16, 8, 128)[:, 4 * g + q] = tiles[q].astype(BF16)
+    exchange(sb6, rb6, 7)
 
     out_part = dot(grad_p[pl.ds(0, 128)], grad_po[...], NT)
     gate_part = dot(normed[...], grad_p[pl.ds(512, 128)], NT)
@@ -313,29 +306,33 @@
     sums[:, 5, :] = out_part
     sums[:, 7, :] = jnp.broadcast_to(gain_out_part, (128, 128))
 
-    def edge_grads(dr):
-        first = pl.multiple_of(lax.rem(rx + 8 - dr, 8) * 16, 16)
+    def edge_grads(buffer, gate, r):
+        first = pl.multiple_of(r * 16, 16)
         here = pl.ds(first, 16)
-        wide[here] = rb4[here].astype(F32)
+        wide[here, 0:8, :] = buffer[here].astype(F32)
         for s in range(8):
             lanes = pl.ds(s * 128, 128)
-            gl, gr = wide[here, s, :], wide[here, 8 + s, :]
-            s0, p1 = gates[0, here, lanes], gates[1, here, lanes]
-            s2, p3 = gates[2, here, lanes], gates[3, here, lanes]
-            dl, dr_ = gl * s0, gr * s2
-            grad_p[here, lanes] = (dl * p1 * (1.0 - s0)).astype(BF16)
-            grad_p[pl.ds(128 + first, 16), lanes] = dl.astype(BF16)
-            grad_p[pl.ds(256 + first, 16), lanes] = (dr_ * p3 * (1.0 - s2)).astype(BF16)
-            grad_p[pl.ds(384 + first, 16), lanes] = dr_.astype(BF16)
-
-    def edge_grad_group(dr, carry):
+            sig, value = gates[gate, here, lanes], gates[gate + 1, here, lanes]
+            grad = wide[here, s, :] * sig
+            grad_p[pl.ds(128 * gate + first, 16), lanes] = (grad * value * (1.0 - sig)).astype(BF16)
+            grad_p[pl.ds(128 * gate + 128 + first, 16), lanes] = grad.astype(BF16)
+
+    def left_group(dr, carry):
         drain(rb4, 16, recv.at[3, dr])
-        edge_grads(dr)
+        edge_grads(rb4, 0, lax.rem(rx + dr, 8))
+        return carry
+
+    def right_group(dr, carry):
+        drain(rb6, 16, recv.at[7, dr])
+        edge_grads(rb6, 2, lax.rem(rx + 8 - dr, 8))
         return carry
 
     drain(rb4, 15, recv.at[3, 0])
-    edge_grads(0)
-    lax.fori_loop(1, 8, edge_grad_group, 0)
+    edge_grads(rb4, 0, rx)
+    lax.fori_loop(1, 8, left_group, 0)
+    drain(rb6, 15, recv.at[7, 0])
+    edge_grads(rb6, 2, rx)
+    lax.fori_loop(1, 8, right_group, 0)
     gain_sum = jnp.zeros((128, 128), F32)
     for s in range(8):
         lanes = pl.ds(s * 128, 128)
@@ -391,9 +388,11 @@
     along_plane(lambda p: total_bf, final.at[rows_of(spot)], 6)
     final[rows_of(spot)] = total_bf[...]
     drain(sb1, 127, send.at[0])
+    drain(sb0, 127, send.at[8])
     drain(rb2, 127, send.at[1])
     drain(sb3, 127, send.at[2])
     drain(rb4, 127, send.at[3])
+    drain(rb6, 127, send.at[7])
     drain(rb5, 31, send.at[4])
     drain(planes, 7, send.at[5])
     drain(rb5, 31, send.at[6])
@@ -429,8 +428,10 @@
         ((1, 128), F32),
         ((1, 128), F32),
         ((128, 16, 128), F32),
-        ((128, 16, 128), BF16),
-        ((128, 16, 128), BF16),
+        ((128, 8, 128), BF16),
+        ((128, 8, 128), BF16),
+        ((128, 8, 128), BF16),
+        ((128, 8, 128), BF16),
         ((2, 2, 8, 32, 512), BF16),
         ((128, 8, 128), BF16),
         ((128, 8, 128), BF16),
@@ -438,8 +439,10 @@
         ((128, 8, 128), BF16),
         ((2, 8, 32, 256), BF16),
         ((8, 32, 256), BF16),
-        ((128, 16, 128), BF16),
-        ((128, 16, 128), BF16),
+        ((128, 8, 128), BF16),
+        ((128, 8, 128), BF16),
+        ((128, 8, 128), BF16),
+        ((128, 8, 128), BF16),
         ((128, 1024), BF16),
         ((128, 1024), F32),
         ((1, 1024), F32),
@@ -482,8 +485,8 @@
         scratch_shapes=[pltpu.VMEM(shape, kind) for shape, kind in scratch]
         + [
             pltpu.SemaphoreType.DMA((6,)),
-            pltpu.SemaphoreType.DMA((7,)),
-            pltpu.SemaphoreType.DMA((7, 8)),
+            pltpu.SemaphoreType.DMA((9,)),
+            pltpu.SemaphoreType.DMA((9, 8)),
             pltpu.SemaphoreType.DMA((3,)),
             pltpu.SemaphoreType.DMA((3,)),
         ],

time: 88.1 us -> 83.7 us (0.950)
  Pallas kernels: 87.4 us -> 83 us
    pallas_call x1, Pallas kernels: 86.3 us -> 82 us  [on_device(): pl.pallas_call(kernel, out_shape=shapes, in_specs=[hbm] * 6, out_specs=[v...]
where the time goes in v4:
time: 83.7 us
  Pallas kernels  83 us (99%)
    pallas_call x1, Pallas kernels, on_device(): pl.pallas_call(kernel, out_shape=shapes, in_specs=[hbm] * 6, out_specs=[v...  82 us

profile of v4, /device:TPU:1, one launch (start us, length us, event | category | flops | bytes accessed | tf_op | source)
XLA Modules:
  0.0 83.7 jit_solution(12637566060321397758)
XLA Ops:
  0.6 82.0 %shard_map.101 = (bf16[4,8,32,128]{3,2,1,0:T(8,128)(2,1)S(1)}, f32[4,8,32,128]{3,2,1,0:T(8,128)S(1)}, f32[128,640]{1,0:T(8,128)S(1)}, f32[128,128]{1,0:T(8,128)S(1)}, f32[2,128]{1,0:T(2,128)S(1)}) custom-call(bf16[4,8,32,128]{3,2,1,0:T(8,128)(2,1)} %bitcast.6, f32[1,128]{1,0:T(1,128)} %bitcast.8, bf16[128,640]{1,0:T(8,128)(2,1)} %weight_h.1, ...), custom_call_target="tpu_custom_call" | custom-call | tf_op jit(solution)/shard_map/pallas_call | solution.py:480
  82.6 1.0 %shard_map.102 = (bf16[4,8,32,128]{3,2,1,0:T(8,128)(2,1)}, f32[4,8,32,128]{3,2,1,0:T(8,128)}, f32[128,640]{1,0:T(8,128)}, f32[128,128]{1,0:T(8,128)}, f32[2,128]{1,0:T(2,128)}) custom-call(bf16[4,8,32,128]{3,2,1,0:T(8,128)(2,1)S(1)} %get-tuple-element.15.refs_0_, f32[4,8,32,128]{3,2,1,0:T(8,128)S(1)} %get-tuple-element.16.refs_1_, ...), custom_call_target="tpu_custom_call" | custom-call | tf_op jit(solution)/shard_map/pallas_call | solution.py:497

commit v5 on v4

--- a/solution.py
+++ b/solution.py
@@ -6,6 +6,7 @@
 from jax.sharding import PartitionSpec as P
 
 EPS = 1e-05
+SPAN = 2
 MESH = pl.DeviceIdType.MESH
 F32 = jnp.float32
 BF16 = jnp.bfloat16
@@ -40,7 +41,7 @@
     pair_h, gain_in_h, weight_h, gain_out_h, out_weight_h, out_grad_h,
     update_o, pair_grad_o, weight_grad_o, out_weight_grad_o, gain_grad_o,
     pair, weight, out_weight, out_grad, gain_in, gain_out,
-    wide, sb0, rb0, sb1, rb1, edges, sb2, rb2, sb3, rb3, grad_mat, grad_far, sb4, rb4, sb6, rb6,
+    wide, sb0, rb0, sb1, rb1, edges, right_t, sb2, rb2, sb3, rb3, grad_mat, grad_far, sb4, rb4, sb6, rb6,
     normed, hat_in, rstd_in, gates, grad_po, grad_no, og_t, grad_p, w_t, ow_t, g_in, g_out,
     sb5, rb5, sums, plane_sum, planes, total_bf, final,
     load, send, recv, sib_send, sib_recv,
@@ -169,6 +170,60 @@
     exchange(sb1, rb1, 0)
     exchange(sb0, rb0, 8)
 
+    def side_of(slot, side):
+        return edges[slot, side].reshape(256, 512)
+
+    def place(slot):
+        return core if slot == 0 else 1 - core
+
+    def edge_rows(buffer, side, r):
+        parts = []
+        for g in range(4):
+            parts.append(swap_blocks([buffer[r * 16 + 4 * g + q].astype(F32) for q in range(4)]))
+        rows = [jnp.concatenate([parts[g][a] for g in range(4)], axis=1) for a in range(4)]
+        edges[0, side, r] = jnp.concatenate(rows, axis=0).astype(BF16)
+        to_sibling(edges.at[0, side, r], edges.at[1, side, r], side).start()
+
+    def right_group(dr, carry):
+        drain(rb1, 16, recv.at[0, dr])
+        edge_rows(rb1, 1, lax.rem(rx + 8 - dr, 8))
+        return carry
+
+    drain(rb1, 15, recv.at[0, 0])
+    edge_rows(rb1, 1, rx)
+    lax.fori_loop(1, 8, right_group, 0)
+    to_sibling(edges.at[0, 1], edges.at[1, 1], 1).wait_recv()
+
+    for slot in range(2):
+        right_t[:, pl.ds(256 * slot, 256)] = side_of(slot, 1).astype(F32).T.astype(BF16)
+
+    def behind(dr):
+        return lax.rem(rx + 8 - dr, 8)
+
+    def send_mixed(start, first):
+        near = [(start + i, behind(start + i)) for i in range(SPAN)]
+        for i, (dr, r) in enumerate(near):
+            drain(rb0, 15 if first and i == 0 else 16, recv.at[8, dr])
+            edge_rows(rb0, 0, r)
+        every = dot(jnp.concatenate([edges[0, 0, r] for _, r in near], axis=0), right_t[...])
+        for i, (dr, r) in enumerate(near):
+            rows = every[32 * i : 32 * i + 32]
+            for slot in range(2):
+                for g in range(2):
+                    lanes = slice(slot * 256 + g * 128, slot * 256 + g * 128 + 128)
+                    tiles = swap_blocks([rows[8 * a : 8 * a + 8, lanes] for a in range(4)])
+                    for q in range(4):
+                        sb2[r * 16 + 2 * (4 * g + q) + place(slot)] = tiles[q].astype(BF16)
+            send_row(sb2, rb2, 1, dr, r, 1 if first and i == 0 else 0)
+
+    def mixed_group(step, carry):
+        send_mixed(step * SPAN, False)
+        return carry
+
+    send_mixed(0, True)
+    rb2[me] = sb2[me]
+    lax.fori_loop(1, 8 // SPAN, mixed_group, 0)
+
     loads[2].wait()
     loads[3].wait()
     ow_t[...] = out_weight[...].astype(F32).T.astype(BF16)
@@ -182,49 +237,6 @@
         grad_po[:, lanes] = gpo
         grad_no[:, lanes] = dot(out_weight[...], gpo)
 
-    def side_of(slot, side):
-        return edges[slot, side].reshape(256, 512)
-
-    def place(slot):
-        return core if slot == 0 else 1 - core
-
-    def edge_rows(buffer, side, r):
-        parts = []
-        for g in range(4):
-            parts.append(swap_blocks([buffer[r * 16 + 4 * g + q].astype(F32) for q in range(4)]))
-        rows = [jnp.concatenate([parts[g][a] for g in range(4)], axis=1) for a in range(4)]
-        edges[0, side, r] = jnp.concatenate(rows, axis=0).astype(BF16)
-        to_sibling(edges.at[0, side, r], edges.at[1, side, r], side).start()
-
-    def right_group(dr, carry):
-        drain(rb1, 16, recv.at[0, dr])
-        edge_rows(rb1, 1, lax.rem(rx + 8 - dr, 8))
-        return carry
-
-    drain(rb1, 15, recv.at[0, 0])
-    edge_rows(rb1, 1, rx)
-    lax.fori_loop(1, 8, right_group, 0)
-    to_sibling(edges.at[0, 1], edges.at[1, 1], 1).wait_recv()
-
-    def send_mixed(dr, r, first):
-        edge_rows(rb0, 0, r)
-        for slot in range(2):
-            rows = dot(edges[0, 0, r], side_of(slot, 1), NT)
-            for g in range(2):
-                tiles = swap_blocks([rows[8 * a : 8 * a + 8, g * 128 : g * 128 + 128] for a in range(4)])
-                for q in range(4):
-                    sb2[r * 16 + 2 * (4 * g + q) + place(slot)] = tiles[q].astype(BF16)
-        send_row(sb2, rb2, 1, dr, r, first)
-
-    def mixed_group(dr, carry):
-        drain(rb0, 16, recv.at[8, dr])
-        send_mixed(dr, lax.rem(rx + 8 - dr, 8), 0)
-        return carry
-
-    drain(rb0, 15, recv.at[8, 0])
-    send_mixed(0, rx, 1)
-    rb2[me] = sb2[me]
-    lax.fori_loop(1, 8, mixed_group, 0)
     arrive(rb2, 1)
 
     wide[:, 0:8, :] = rb2[...].astype(F32)
@@ -245,16 +257,6 @@
     sb3[...] = wide[:, 8:16, :].astype(BF16)
     exchange(sb3, rb3, 2)
 
-    gain_out_part = jnp.sum(gain_sum.T, axis=0, keepdims=True)
-    for s in range(8):
-        lanes = pl.ds(s * 128, 128)
-        no = (grad_no[:, lanes] * g_out[...]).astype(BF16)
-        grad_p[pl.ds(0, 128), lanes] = no
-        po = dot(ow_t[...], no)
-        gate = gates[4, :, lanes]
-        update_o[:, s] = (gate * po).T.reshape(4, 32, 128).astype(BF16)
-        grad_p[pl.ds(512, 128), lanes] = (og_t[:, lanes] * po * (gate * (1.0 - gate))).astype(BF16)
-
     def grad_rows(dr):
         r = lax.rem(rx + 8 - dr, 8)
         for slot in range(2):
@@ -267,31 +269,33 @@
             grad_mat[slot, r] = jnp.concatenate(rows, axis=0).astype(BF16)
         to_sibling(grad_mat.at[1, r], grad_far.at[r], 2).start()
 
-    def send_left(dr, first):
-        r = lax.rem(rx + 8 - dr, 8)
-        rows = dot(grad_mat[0, r], side_of(0, 1)) + dot(grad_mat[1, r], side_of(1, 1))
-        for g in range(4):
-            tiles = swap_blocks([rows[8 * a : 8 * a + 8, g * 128 : g * 128 + 128] for a in range(4)])
-            for q in range(4):
-                sb4[r * 16 + 4 * g + q] = tiles[q].astype(BF16)
-
-        send_row(sb4, rb4, 3, dr, r, first)
-
-    drain(sb3, 15, recv.at[2, 0])
-    grad_rows(0)
-    send_left(0, 1)
+    def send_left(start, first):
+        near = [(start + i, behind(start + i)) for i in range(SPAN)]
+        for i, (dr, r) in enumerate(near):
+            drain(sb3, 15 if first and i == 0 else 16, recv.at[2, dr])
+            grad_rows(dr)
+        every = sum(
+            dot(jnp.concatenate([grad_mat[slot, r] for _, r in near], axis=0), side_of(slot, 1))
+            for slot in range(2)
+        )
+        for i, (dr, r) in enumerate(near):
+            rows = every[32 * i : 32 * i + 32]
+            for g in range(4):
+                tiles = swap_blocks([rows[8 * a : 8 * a + 8, g * 128 : g * 128 + 128] for a in range(4)])
+                for q in range(4):
+                    sb4[r * 16 + 4 * g + q] = tiles[q].astype(BF16)
+            send_row(sb4, rb4, 3, dr, r, 1 if first and i == 0 else 0)
+
+    def left_rows(step, carry):
+        send_left(step * SPAN, False)
+        return carry
+
+    send_left(0, True)
     rb4[me] = sb4[me]
-
-    def grad_group(dr, carry):
-        drain(sb3, 16, recv.at[2, dr])
-        grad_rows(dr)
-        send_left(dr, 0)
-        return carry
-
-    lax.fori_loop(1, 8, grad_group, 0)
+    lax.fori_loop(1, 8 // SPAN, left_rows, 0)
     to_sibling(edges.at[0, 0], edges.at[1, 0], 0).wait_recv()
-    near = grad_mat[0].reshape(256, 256)
-    grad_right = dot(near, side_of(0, 0), TN)
+    mine = grad_mat[0].reshape(256, 256)
+    grad_right = dot(mine, side_of(0, 0), TN)
     to_sibling(grad_mat.at[1], grad_far, 2).wait_recv()
     grad_right = (grad_right + dot(grad_far[...].reshape(256, 256), side_of(1, 0), TN)).reshape(8, 4, 8, 512)
     for g in range(4):
@@ -300,6 +304,15 @@
             sb6.reshape(8, 16, 8, 128)[:, 4 * g + q] = tiles[q].astype(BF16)
     exchange(sb6, rb6, 7)
 
+    gain_out_part = jnp.sum(gain_sum.T, axis=0, keepdims=True)
+    for s in range(8):
+        lanes = pl.ds(s * 128, 128)
+        no = (grad_no[:, lanes] * g_out[...]).astype(BF16)
+        grad_p[pl.ds(0, 128), lanes] = no
+        po = dot(ow_t[...], no)
+        gate = gates[4, :, lanes]
+        update_o[:, s] = (gate * po).T.reshape(4, 32, 128).astype(BF16)
+        grad_p[pl.ds(512, 128), lanes] = (og_t[:, lanes] * po * (gate * (1.0 - gate))).astype(BF16)
     out_part = dot(grad_p[pl.ds(0, 128)], grad_po[...], NT)
     gate_part = dot(normed[...], grad_p[pl.ds(512, 128)], NT)
     sums[:, 4, :] = gate_part
@@ -433,6 +446,7 @@
         ((128, 8, 128), BF16),
         ((128, 8, 128), BF16),
         ((2, 2, 8, 32, 512), BF16),
+        ((512, 512), BF16),
         ((128, 8, 128), BF16),
         ((128, 8, 128), BF16),
         ((128, 8, 128), BF16),

time: 83.7 us -> 82.9 us (level)
    pallas_call x1, Pallas kernels: 82 us -> 81.1 us  [on_device(): pl.pallas_call(kernel, out_shape=shapes, in_specs=[hbm] * 6, out_specs=[v...]
where the time goes in v5:
time: 82.9 us; the launch traced here: 82.8 us
  Pallas kernels  82.2 us (99%)
    pallas_call x1, Pallas kernels, on_device(): pl.pallas_call(kernel, out_shape=shapes, in_specs=[hbm] * 6, out_specs=[v...  81.1 us

profile of v5, /device:TPU:1, one launch (start us, length us, event | category | flops | bytes accessed | tf_op | source)
XLA Modules:
  0.0 82.8 jit_solution(13685749717859341149)
XLA Ops:
  0.6 81.1 %shard_map.101 = (bf16[4,8,32,128]{3,2,1,0:T(8,128)(2,1)S(1)}, f32[4,8,32,128]{3,2,1,0:T(8,128)S(1)}, f32[128,640]{1,0:T(8,128)S(1)}, f32[128,128]{1,0:T(8,128)S(1)}, f32[2,128]{1,0:T(2,128)S(1)}) custom-call(bf16[4,8,32,128]{3,2,1,0:T(8,128)(2,1)} %bitcast.6, f32[1,128]{1,0:T(1,128)} %bitcast.8, bf16[128,640]{1,0:T(8,128)(2,1)} %weight_h.1, ...), custom_call_target="tpu_custom_call" | custom-call | tf_op jit(solution)/shard_map/pallas_call | solution.py:494
  81.8 1.0 %shard_map.102 = (bf16[4,8,32,128]{3,2,1,0:T(8,128)(2,1)}, f32[4,8,32,128]{3,2,1,0:T(8,128)}, f32[128,640]{1,0:T(8,128)}, f32[128,128]{1,0:T(8,128)}, f32[2,128]{1,0:T(2,128)}) custom-call(bf16[4,8,32,128]{3,2,1,0:T(8,128)(2,1)S(1)} %get-tuple-element.15.refs_0_, f32[4,8,32,128]{3,2,1,0:T(8,128)S(1)} %get-tuple-element.16.refs_1_, ...), custom_call_target="tpu_custom_call" | custom-call | tf_op jit(solution)/shard_map/pallas_call | solution.py:511

commit v6 on v5

--- a/solution.py
+++ b/solution.py
@@ -71,8 +71,19 @@
         line(0, 1)
         lax.fori_loop(1, 8, rest, 0)
 
-    def greet(dr, r, c):
-        pl.semaphore_signal(barrier, inc=1, device_id=(r * 2 + core, c), device_id_type=MESH)
+    def greet_far_first():
+        x, y = lax.div(rx, 2), lax.div(col, 8) * 2 + lax.rem(rx, 2)
+        xs = [lax.rem(x + 2 + i, 4) * 4 + core for i in range(4)]
+        ys = [lax.rem(y + 2 + i, 4) for i in range(4)]
+        lines = [(lax.rem(v, 2) * 2, lax.div(v, 2) * 8) for v in ys]
+        for pair_z in ((4,), (3, 5), (2, 6), (1, 7), (0,)):
+            for k in range(16):
+                if pair_z == (0,) and k == 10:
+                    continue
+                r, c = xs[k // 4] + lines[k % 4][0], lines[k % 4][1]
+                for dz in pair_z:
+                    device = (r, c + lax.rem(z + dz, 8))
+                    pl.semaphore_signal(barrier, inc=1, device_id=device, device_id_type=MESH)
 
     loads = [
         pltpu.make_async_copy(source, target, load.at[i])
@@ -85,7 +96,7 @@
     ]
     for copy in loads:
         copy.start()
-    partners(greet)
+    greet_far_first()
 
     def in_plane(d):
         p = lax.rem(spot + d, 32)
@@ -343,19 +354,27 @@
     drain(rb4, 15, recv.at[3, 0])
     edge_grads(rb4, 0, rx)
     lax.fori_loop(1, 8, left_group, 0)
+    for s in range(8):
+        lanes = pl.ds(s * 128, 128)
+        og_t[:, lanes] = dot(weight[:, 0:256], grad_p[pl.ds(0, 256), lanes]) + dot(
+            weight[:, 512:640], grad_p[pl.ds(512, 128), lanes]
+        )
+    in_part = dot(normed[...], grad_p[pl.ds(0, 256)], NT)
+    for b in range(2):
+        sums[:, b, :] = in_part[:, b * 128 : b * 128 + 128]
     drain(rb6, 15, recv.at[7, 0])
     edge_grads(rb6, 2, rx)
     lax.fori_loop(1, 8, right_group, 0)
     gain_sum = jnp.zeros((128, 128), F32)
     for s in range(8):
         lanes = pl.ds(s * 128, 128)
-        gni = dot(weight[...], grad_p[:, lanes])
+        gni = og_t[:, lanes] + dot(weight[:, 256:512], grad_p[pl.ds(256, 256), lanes])
         gain_sum = gain_sum + gni * hat_in[:, lanes]
         og_t[:, lanes] = gni
     gain_in_part = jnp.sum(gain_sum.T, axis=0, keepdims=True)
-    in_part = dot(normed[...], grad_p[pl.ds(0, 512)], NT)
-    for b in range(4):
-        sums[:, b, :] = in_part[:, b * 128 : b * 128 + 128]
+    in_part = dot(normed[...], grad_p[pl.ds(256, 256)], NT)
+    for b in range(2):
+        sums[:, 2 + b, :] = in_part[:, b * 128 : b * 128 + 128]
     sums[:, 6, :] = jnp.broadcast_to(gain_in_part, (128, 128))
 
     def along_plane(source, target, slot):

time: 82.9 us -> 81.8 us (0.987)
  Pallas kernels: 82.2 us -> 81.1 us
    pallas_call x1, Pallas kernels: 81.1 us -> 80 us  [on_device(): pl.pallas_call(kernel, out_shape=shapes, in_specs=[hbm] * 6, out_specs=[v...]
where the time goes in v6:
time: 81.8 us; the launch traced here: 81.7 us
  Pallas kernels  81.1 us (99%)
    pallas_call x1, Pallas kernels, on_device(): pl.pallas_call(kernel, out_shape=shapes, in_specs=[hbm] * 6, out_specs=[v...  80 us

profile of v6, /device:TPU:1, one launch (start us, length us, event | category | flops | bytes accessed | tf_op | source)
XLA Modules:
  0.0 81.7 jit_solution(15091056904985256009)
XLA Ops:
  0.6 80.0 %shard_map.101 = (bf16[4,8,32,128]{3,2,1,0:T(8,128)(2,1)S(1)}, f32[4,8,32,128]{3,2,1,0:T(8,128)S(1)}, f32[128,640]{1,0:T(8,128)S(1)}, f32[128,128]{1,0:T(8,128)S(1)}, f32[2,128]{1,0:T(2,128)S(1)}) custom-call(bf16[4,8,32,128]{3,2,1,0:T(8,128)(2,1)} %bitcast.6, f32[1,128]{1,0:T(1,128)} %bitcast.8, bf16[128,640]{1,0:T(8,128)(2,1)} %weight_h.1, ...), custom_call_target="tpu_custom_call" | custom-call | tf_op jit(solution)/shard_map/pallas_call | solution.py:513
  80.7 1.0 %shard_map.102 = (bf16[4,8,32,128]{3,2,1,0:T(8,128)(2,1)}, f32[4,8,32,128]{3,2,1,0:T(8,128)}, f32[128,640]{1,0:T(8,128)}, f32[128,128]{1,0:T(8,128)}, f32[2,128]{1,0:T(2,128)}) custom-call(bf16[4,8,32,128]{3,2,1,0:T(8,128)(2,1)S(1)} %get-tuple-element.15.refs_0_, f32[4,8,32,128]{3,2,1,0:T(8,128)S(1)} %get-tuple-element.16.refs_1_, ...), custom_call_target="tpu_custom_call" | custom-call | tf_op jit(solution)/shard_map/pallas_call | solution.py:530
